TPU v7x, 256 devices: a whole 4x4x8 slice. The times are simulated.
256 devices in a mesh: pos: 16 (over x, z_lo), tile: 16 (over y, z_hi, core).
Axes of the slice: x: 4, y: 4, z: 8 (z_hi: 2, z_lo: 4; z = z_hi * 4 + z_lo), core: 2. Of those that a mesh axis runs over, the one named last changes fastest.
Arguments:
- object_slices: bfloat16 [16, 2, 2, 128, 1024], P('tile', None, None, 'pos'), may hold values from -4 to 4
- probe_modes: float32 [8, 2, 128, 128], replicated, may hold values from -4 to 4
- offsets: int32 [16, 16, 4, 2], P('tile', 'pos'), may hold values from 0 to 896, as said below
- counts: int32 [16, 16], P('tile', 'pos'), may hold values from 1 to 4, 32 in all within a row
- patterns: float32 [16, 16, 4, 128, 128], P('tile', 'pos'), may hold values from 0.05 to 36
Outputs:
- object_grad: float32 [16, 2, 2, 128, 1024], P('tile', None, None, 'pos')
- probe_grad: float32 [8, 2, 128, 128], replicated
Inputs may be any that keep to these rules, and one draw needn't show every extreme that they name: `offsets`: entry 0 is a slot's row offset within its region's tile, and 0 in the last tile; entry 1 its column offset; so every footprint lies inside the object and reaches at most into the next tile. A device's live slots are its first counts slots; the counts of every region add up to 32.
All inputs are finite; a program needn't handle non-finite values.
Results may differ from a plain program's by a relative error of at most 0.0003.
Values may be sent and summed in bfloat16 or wider, within the bound.
A program may use at most 64 MiB of HBM per device.

v0:
```python
from functools import partial
import math

import jax
import jax.numpy as jnp
from jax import lax
from jax.sharding import PartitionSpec as P

fresnel_coef = 24.0
highest = lax.Precision.HIGHEST


def from_behind(block, axis, distance):
    devices = range(lax.axis_size(axis))
    route = [(i - distance, i) for i in devices if i - distance in devices]
    return lax.ppermute(block, axis, route)


def dft_tables(length):
    indices = jnp.arange(length, dtype=jnp.int32)
    product = indices[:, None] * indices[None, :] % length
    angle = 2.0 * math.pi / length * product.astype(jnp.float32)
    factor = 1.0 / math.sqrt(length)
    return (jnp.cos(angle) * factor, -jnp.sin(angle) * factor)


def fresnel_kernel(length):
    indices = jnp.arange(length, dtype=jnp.int32)
    frequency = ((indices + length // 2) % length - length // 2).astype(jnp.float32) / length
    phase = -jnp.pi * fresnel_coef * (frequency[:, None] ** 2 + frequency[None, :] ** 2)
    return jnp.stack([jnp.cos(phase), jnp.sin(phase)])


def transform(field, real_table, imag_table):
    right_real = jnp.einsum("mcjk,kl->mcjl", field, real_table, precision=highest)
    right_imag = jnp.einsum("mcjk,kl->mcjl", field, imag_table, precision=highest)
    half = jnp.stack(
        [right_real[:, 0] - right_imag[:, 1], right_imag[:, 0] + right_real[:, 1]], axis=1
    )
    left_real = jnp.einsum("ij,mcjl->mcil", real_table, half, precision=highest)
    left_imag = jnp.einsum("ij,mcjl->mcil", imag_table, half, precision=highest)
    return jnp.stack([left_real[:, 0] - left_imag[:, 1], left_imag[:, 0] + left_real[:, 1]], axis=1)


def multiply(field, factor):
    real_part = field[:, 0] * factor[0] - field[:, 1] * factor[1]
    imag_part = field[:, 0] * factor[1] + field[:, 1] * factor[0]
    return jnp.stack([real_part, imag_part], axis=1)


def position_loss(probe_modes, window, measured, tables, kernel):
    real_table, imag_table = tables
    wavefield = multiply(probe_modes, window[0])
    spectrum = multiply(transform(wavefield, real_table, imag_table), kernel)
    wavefield = multiply(transform(spectrum, real_table, -imag_table), window[1])
    far_field = transform(wavefield, real_table, imag_table)
    intensity = jnp.sum(far_field[:, 0] ** 2 + far_field[:, 1] ** 2, axis=0)
    return 0.5 * jnp.sum((intensity - measured) ** 2)


def slot_terms(window, measured_one, live_one, probe_modes, tables, kernel):

    def loss_of(probe_arg, window_arg):
        return live_one * position_loss(probe_arg, window_arg, measured_one, tables, kernel)

    loss_value, pullback = jax.vjp(loss_of, probe_modes, window)
    return pullback(jnp.ones_like(loss_value))


def add_position(carry, inputs, extended, probe_modes, tables, kernel):
    object_grad, probe_grad = carry
    row_one, col_one, measured_one, live_one = inputs
    patch_side = probe_modes.shape[-1]
    zero_index = jnp.zeros((), jnp.int32)
    starts = (zero_index, zero_index, row_one, col_one)
    window_shape = (extended.shape[0], 2, patch_side, patch_side)
    window = lax.dynamic_slice(extended, starts, window_shape)
    probe_term, window_term = slot_terms(
        window, measured_one, live_one, probe_modes, tables, kernel
    )
    current = lax.dynamic_slice(object_grad, starts, window_shape)
    object_grad = lax.dynamic_update_slice(object_grad, current + window_term, starts)
    return ((object_grad, probe_grad + probe_term), None)


def per_device(object_slices, probe_modes, offsets, counts, patterns):
    patch_side = probe_modes.shape[-1]
    slot_count = offsets.shape[2]
    tables = dft_tables(patch_side)
    kernel = fresnel_kernel(patch_side)
    chosen_offsets = offsets[0, 0]
    chosen_patterns = patterns[0, 0]
    live_mask = (jnp.arange(slot_count, dtype=jnp.int32) < counts[0, 0]).astype(jnp.float32)
    own_tile = lax.all_gather(object_slices, "pos", axis=3, tiled=True)
    next_tile = from_behind(own_tile, "tile", -1)
    extended = jnp.concatenate([own_tile[0], next_tile[0]], axis=2).astype(jnp.float32)
    stepper = partial(
        add_position, extended=extended, probe_modes=probe_modes, tables=tables, kernel=kernel
    )
    initial = (jnp.zeros(extended.shape, jnp.float32), jnp.zeros(probe_modes.shape, jnp.float32))
    scanned = (chosen_offsets[:, 0], chosen_offsets[:, 1], chosen_patterns, live_mask)
    (object_grad, probe_grad), unused = lax.scan(stepper, initial, scanned)
    own_part = object_grad[None, :, :, :patch_side]
    next_part = object_grad[None, :, :, patch_side:]
    moved = from_behind(next_part, "tile", 1)
    object_out = lax.psum_scatter(own_part + moved, "pos", scatter_dimension=3, tiled=True)
    probe_out = lax.psum(probe_grad, ("pos", "tile"))
    return (object_out, probe_out)


def solution(mesh):
    placed = (
        P("tile", None, None, "pos", None),
        P(),
        P("tile", "pos", None, None),
        P("tile", "pos"),
        P("tile", "pos", None, None, None),
    )
    return jax.shard_map(
        per_device,
        mesh=mesh,
        in_specs=placed,
        out_specs=(P("tile", None, None, "pos", None), P()),
        check_vma=False,
    )
```

profile of v0, /device:TPU:1, one launch (start us, length us, event | category | flops | bytes accessed | tf_op | source)
XLA Modules:
  0.0 772.3 jit_solution(3860463136490187178)
XLA Ops:
  7.9 78.0 %all-gather.2.cloned.1.call-done = bf16[1,2,2,128,1024]{4,3,2,1,0:T(8,128)(2,1)} async-done(((bf16[1,2,2,8,1024]{4,3,2,1,0:T(8,128)(2,1)}), bf16[1,2,2,128,1024]{4,3,2,1,0:T(8,128)(2,1)}) %all-gather.2.cloned.1.call-update) | async-done | bytes 1048592 | tf_op jit(solution)/shard_map/all_gather | solution.py:94
  86.0 12.3 %collective-permute-start = (bf16[1,2,2,128,1024]{4,3,2,1,0:T(8,128)(2,1)}, bf16[1,2,2,128,1024]{4,3,2,1,0:T(8,128)(2,1)}, u32[]{:S(2)}, u32[]{:S(2)}) collective-permute-start(bf16[1,2,2,128,1024]{4,3,2,1,0:T(8,128)(2,1)} %all-gather.2.cloned.1.call-done), channel_id=1, source_target_pairs={{1,0},{2,1},{3,2},{4,3},{5,4},{6,5},{7,6},{8,7},{9,8},{10,9},{11,1... | collective-permute-start | bytes 3145736 | tf_op jit(solution)/shard_map/ppermute | solution.py:16
  102.7 13.7 %collective-permute-done = bf16[1,2,2,128,1024]{4,3,2,1,0:T(8,128)(2,1)} collective-permute-done((bf16[1,2,2,128,1024]{4,3,2,1,0:T(8,128)(2,1)}, bf16[1,2,2,128,1024]{4,3,2,1,0:T(8,128)(2,1)}, u32[]{:S(2)}, u32[]{:S(2)}) %collective-permute-start) | collective-permute-done | bytes 1048608 | tf_op jit(solution)/shard_map/ppermute | solution.py:16
  116.4 4.0 maximum_convert_fusion
  120.3 2.5 broadcast_in_dim.82.clone
  122.8 275.5 %while.18 = (s32[]{:T(128)}, f32[2,2,256,1024]{3,2,1,0:T(8,128)}, f32[8,2,128,128]{3,2,1,0:T(8,128)S(1)}, s32[4]{0:T(128)S(1)}, s32[4]{0:T(128)S(1)}, /*index=5*...) while((s32[]{:T(128)}, f32[2,2,256,1024]{3,2,1,0:T(8,128)}, ...), condition=%wide.region_10.11_spmd.clone.clone.clone.clone, body=%wide.region_0.10_spmd.clone.clone.clone.clone.sunk | while | flops 9693036544 | bytes 139133840 | solution.py:102
  143.0 2.5 convolution_bitcast_fusion.15
  149.6 2.0 fusion.389
  187.1 3.5 dynamic_update_slice.11
  211.2 2.1 convolution_bitcast_fusion.15
  217.5 2.0 fusion.389
  255.1 4.3 dynamic_update_slice.11
  279.8 2.1 convolution_bitcast_fusion.15
  286.1 2.0 fusion.389
  323.7 4.3 dynamic_update_slice.11
  348.5 2.3 convolution_bitcast_fusion.15
  392.4 4.2 dynamic_update_slice.11
  398.3 3.5 slice_bitcast_fusion
  401.8 2.2 collective-permute-start.1
  404.1 44.1 %collective-permute-done.1 = f32[1,2,2,128,1024]{4,3,2,1,0:T(8,128)} collective-permute-done((f32[1,2,2,128,1024]{4,3,2,1,0:T(8,128)}, f32[1,2,2,128,1024]{4,3,2,1,0:T(8,128)}, u32[]{:S(2)}, u32[]{:S(2)}) %collective-permute-start.1) | collective-permute-done | bytes 2097184 | tf_op jit(solution)/shard_map/ppermute | solution.py:16
  448.2 4.1 bitcast_add_fusion
  452.3 225.9 %all-reduce.44.cloned.1.call-done = f32[8,2,128,128]{3,2,1,0:T(8,128)} async-done(((f32[8,2,128,128]{3,2,1,0:T(8,128)}), f32[8,2,128,128]{3,2,1,0:T(8,128)}) %all-reduce.44.cloned.1.call-update) | async-done | bytes 1048592 | tf_op jit(solution)/shard_map/psum | solution.py:107
  678.3 84.8 %reduce-scatter.2.cloned.1.call-done = f32[1,2,2,8,1024]{4,3,2,1,0:T(8,128)} async-done(((f32[1,2,2,128,1024]{4,3,2,1,0:T(8,128)}), f32[1,2,2,8,1024]{4,3,2,1,0:T(8,128)}) %reduce-scatter.2.cloned.1.call-update) | async-done | bytes 131088 | tf_op jit(solution)/shard_map/reduce_scatter | solution.py:106
  763.1 2.3 copy.247
  (293 shorter events, 228.9 us)
Async XLA Ops:
  7.2 78.8 %all-gather.2.cloned.1.call-start = ((), (), s32[]{:S(2)}) async-start(), calls=%async_computation.1 | async-start | bytes 1114112 | tf_op jit(solution)/shard_map/all_gather | solution.py:94
  7.9 670.4 %all-reduce.44.cloned.1.call-start = ((), (), s32[]{:S(2)}) async-start(), calls=%async_computation.3 | async-start | bytes 2097152 | tf_op jit(solution)/shard_map/psum | solution.py:107
  86.0 30.4 %collective-permute-start = (bf16[1,2,2,128,1024]{4,3,2,1,0:T(8,128)(2,1)}, bf16[1,2,2,128,1024]{4,3,2,1,0:T(8,128)(2,1)}, u32[]{:S(2)}, u32[]{:S(2)}) collective-permute-start(bf16[1,2,2,128,1024]{4,3,2,1,0:T(8,128)(2,1)} %all-gather.2.cloned.1.call-done), channel_id=1, source_target_pairs={{1,0},{2,1},{3,2},{4,3},{5,4},{6,5},{7,6},{8,7},{9,8},{10,9},{11,1... | collective-permute-start | bytes 3145736 | tf_op jit(solution)/shard_map/ppermute | solution.py:16
  116.4 6.5 copy-start.3
  122.8 32.9 %copy-start.1 = (f32[4,128,128]{1,2,0:T(8,128)}, f32[4,128,128]{1,2,0:T(8,128)S(1)}, u32[]{:S(2)}) copy-start(f32[4,128,128]{1,2,0:T(8,128)S(1)} %get-tuple-element.752) | copy-start | bytes 786436 | tf_op jit(solution)/shard_map/while
  186.6 3.9 copy-start.2
  191.0 32.6 %copy-start.1 = (f32[4,128,128]{1,2,0:T(8,128)}, f32[4,128,128]{1,2,0:T(8,128)S(1)}, u32[]{:S(2)}) copy-start(f32[4,128,128]{1,2,0:T(8,128)S(1)} %get-tuple-element.752) | copy-start | bytes 786436 | tf_op jit(solution)/shard_map/while
  254.7 4.7 copy-start.2
  259.6 32.6 %copy-start.1 = (f32[4,128,128]{1,2,0:T(8,128)}, f32[4,128,128]{1,2,0:T(8,128)S(1)}, u32[]{:S(2)}) copy-start(f32[4,128,128]{1,2,0:T(8,128)S(1)} %get-tuple-element.752) | copy-start | bytes 786436 | tf_op jit(solution)/shard_map/while
  323.3 4.8 copy-start.2
  328.2 32.8 %copy-start.1 = (f32[4,128,128]{1,2,0:T(8,128)}, f32[4,128,128]{1,2,0:T(8,128)S(1)}, u32[]{:S(2)}) copy-start(f32[4,128,128]{1,2,0:T(8,128)S(1)} %get-tuple-element.752) | copy-start | bytes 786436 | tf_op jit(solution)/shard_map/while
  391.9 4.7 copy-start.2
  398.3 5.7 copy-start
  401.8 46.4 %collective-permute-start.1 = (f32[1,2,2,128,1024]{4,3,2,1,0:T(8,128)}, f32[1,2,2,128,1024]{4,3,2,1,0:T(8,128)}, u32[]{:S(2)}, u32[]{:S(2)}) collective-permute-start(f32[1,2,2,128,1024]{4,3,2,1,0:T(8,128)} %slice_bitcast_fusion), channel_id=1, source_target_pairs={{0,1},{1,2},{2,3},{3,4},{4,5},{5,6},{6,7},{7,8},{8,9},{9,10},{10,1... | collective-permute-start | bytes 6291464 | tf_op jit(solution)/shard_map/ppermute | solution.py:16
  404.0 359.1 %reduce-scatter.2.cloned.1.call-start = ((), (), s32[]{:S(2)}) async-start(), calls=%async_computation.2 | async-start | bytes 2228224 | tf_op jit(solution)/shard_map/reduce_scatter | solution.py:106
Sparse Core Ops, SparseCore 0:
  9.8 76.1 all-gather.1
  404.2 274.0 all-reduce.43
  681.6 81.5 reduce-scatter.1
where the time goes:
time: 786 us; the launch traced here: 772 us
  waiting for transfers between devices  447 us (57%)
  matrix products  156 us (20%)
  local copies, waits for them, and re-layouts  78 us (10%)
  other arithmetic  41.6 us (5%)
  loops' own time  19.8 us (3%)
  between operations  14.8 us (2%)
  starting transfers between devices  14.6 us (2%)
    psum x1, waiting for transfers between devices, per_device(): probe_out = lax.psum(probe_grad, ('pos', 'tile'))  226 us
    reduce_scatter x1, waiting for transfers between devices, per_device(): lax.psum_scatter(own_part + moved, 'pos', scatter_dimension=3, tiled=True)  84.8 us
    all_gather x1, waiting for transfers between devices, per_device(): own_tile = lax.all_gather(object_slices, 'pos', axis=3, tiled=True)  78 us
    ppermute x2, waiting for transfers between devices, from_behind(): return lax.ppermute(block, axis, route)  57.8 us
    dot_general x24, matrix products, transform(): left_real = jnp.einsum('ij,mcjl->mcil', real_table, half, precision=highest)  39.2 us
    dot_general x24, matrix products, transform(): jnp.einsum('mcjk,kl->mcjl', field, real_table, precision=highest)  39.2 us
    dot_general x24, matrix products, transform(): left_imag = jnp.einsum('ij,mcjl->mcil', imag_table, half, precision=highest)  38.9 us
    dot_general x24, matrix products, transform(): jnp.einsum('mcjk,kl->mcjl', field, imag_table, precision=highest)  38.8 us
  transfers between devices with their start and end apart: 5, of which 5 were waited for; matrix products, arithmetic and copies ran while one was open for 1% of the time, Pallas kernels for 0%

commit v1 on v0

v1 whole, which is shorter than its diff:
```python
import functools
import math

import jax
import jax.numpy as jnp
import ml_dtypes
import numpy as np
from jax import lax
from jax.experimental import pallas as pl
from jax.experimental.pallas import tpu as pltpu
from jax.sharding import PartitionSpec as P

f32 = jnp.float32
bf16 = jnp.bfloat16
MESH = pl.DeviceIdType.MESH
SIDE = 128
PEERS = 16
SLOTS = 4
TILES = 16
ROWS = SLOTS * 32


def signal_all(barrier, targets):
    for target in targets:
        pl.semaphore_signal(barrier, inc=1, device_id=target, device_id_type=MESH)
    pl.semaphore_wait(barrier, len(targets))


def remote(src, dst, send, recv, target):
    return pltpu.make_async_remote_copy(
        src_ref=src, dst_ref=dst, send_sem=send, recv_sem=recv,
        device_id=target, device_id_type=MESH,
    )


def at(pos, tile):
    return {"pos": pos, "tile": tile}


def offset_of(offs, q, j):
    a = offs[q, 0, 2 * j]
    b = offs[q, 0, 2 * j + 1]
    block = lax.div(b, SIDE)
    return a, block, b - block * SIDE


def gather_kernel(off, shard, pieces, offs_out, nxt, own_f, nxt_f, stage, offs, local_sem,
                  off_send, off_recv, nxt_send, nxt_recv, win_send, win_recv):
    me = lax.axis_index("pos")
    tile = lax.axis_index("tile")
    peers = [lax.rem(me + d, PEERS) for d in range(1, PEERS)]
    below = lax.rem(tile + TILES - 1, TILES)
    above = lax.rem(tile + 1, TILES)
    targets = [at(p, tile) for p in peers] + [at(me, below), at(me, above)]
    signal_all(pltpu.get_barrier_semaphore(), targets)

    next_copy = remote(shard, nxt, nxt_send, nxt_recv, at(me, below))
    next_copy.start()
    off_copies = []
    for d in range(1, PEERS):
        copy = remote(off, offs_out.at[me], off_send.at[d], off_recv.at[d], at(peers[d - 1], tile))
        copy.start()
        off_copies.append(copy)
    offs_out[me] = off[...]
    for block in range(8):
        own_f[block] = shard[:, block * SIDE:(block + 1) * SIDE].astype(f32)
    own_f[8] = jnp.zeros((32, SIDE), f32)
    nxt_f[8] = jnp.zeros((32, SIDE), f32)
    for copy in off_copies:
        copy.wait()
    to_smem = pltpu.make_async_copy(offs_out, offs, local_sem)
    to_smem.start()
    next_copy.wait()
    for block in range(8):
        nxt_f[block] = nxt[:, block * SIDE:(block + 1) * SIDE].astype(f32)
    to_smem.wait()

    row = lax.rem(lax.broadcasted_iota(jnp.int32, (32, SIDE), 0), 8) + me * 8
    lane = lax.broadcasted_iota(jnp.int32, (32, SIDE), 1)

    def cut(q):
        for j in range(SLOTS):
            a, block, shift = offset_of(offs, q, j)
            mask = row >= a
            left = jnp.where(mask, own_f[block], nxt_f[block])
            right = jnp.where(mask, own_f[block + 1], nxt_f[block + 1])
            back = lax.rem(SIDE - shift, SIDE)
            both = jnp.where(lane < SIDE - shift, pltpu.roll(left, back, 1), pltpu.roll(right, back, 1))
            stage[q, j * 32:(j + 1) * 32] = both.astype(bf16)

    def window_copy(d):
        q = lax.rem(me + d, PEERS)
        return remote(stage.at[q], pieces.at[me], win_send.at[d], win_recv.at[d], at(q, tile))

    def send(d, carry):
        cut(lax.rem(me + d, PEERS))
        window_copy(d).start()
        return carry

    lax.fori_loop(1, PEERS, send, 0)
    cut(me)
    pieces[me] = stage[me]

    def finish(d, carry):
        window_copy(d).wait()
        return carry

    lax.fori_loop(1, PEERS, finish, 0)


def gather_windows(off, shard):
    vm = pl.BlockSpec(memory_space=pltpu.VMEM)
    dma = pltpu.SemaphoreType.DMA
    return pl.pallas_call(
        gather_kernel,
        out_shape=[
            jax.ShapeDtypeStruct((PEERS, ROWS, SIDE), bf16),
            jax.ShapeDtypeStruct((PEERS, 1, SIDE), jnp.int32),
        ],
        in_specs=[vm, vm],
        out_specs=[vm, vm],
        scratch_shapes=[
            pltpu.VMEM((32, 1024), bf16),
            pltpu.VMEM((9, 32, SIDE), f32),
            pltpu.VMEM((9, 32, SIDE), f32),
            pltpu.VMEM((PEERS, ROWS, SIDE), bf16),
            pltpu.SMEM((PEERS, 1, SIDE), jnp.int32),
            dma, dma((PEERS,)), dma((PEERS,)), dma, dma, dma((PEERS,)), dma((PEERS,)),
        ],
        compiler_params=pltpu.CompilerParams(
            collective_id=0, has_side_effects=True, vmem_limit_bytes=16 << 20
        ),
        name="gather_windows",
    )(off, shard)


def reduce_kernel(offs, gp, probe, out, gout, gin, nacc, nin, cbuf, work, ybuf, work2, xbuf, work3, zbuf,
                  obj_send, obj_recv, nxt_send, nxt_recv, core_send, core_recv,
                  y_send, y_recv, x_send, x_recv, z_send, z_recv):
    me = lax.axis_index("pos")
    tile = lax.axis_index("tile")
    x, zl = lax.div(me, 4), lax.rem(me, 4)
    y, zh, c = lax.div(tile, 4), lax.rem(lax.div(tile, 2), 2), lax.rem(tile, 2)
    z = zh * 4 + zl
    below = lax.rem(tile + TILES - 1, TILES)
    above = lax.rem(tile + 1, TILES)
    partner = at(me, tile + 1 - 2 * c)
    y_of = [lax.rem(y + d, 4) for d in range(4)]
    x_of = [lax.rem(x + d, 4) for d in range(4)]
    z_of = [lax.rem(z + d, 8) for d in range(8)]
    y_peer = [at(me, v * 4 + zh * 2 + c) for v in y_of]
    x_peer = [at(v * 4 + zl, tile) for v in x_of]
    z_peer = [at(x * 4 + lax.rem(v, 4), y * 4 + lax.div(v, 4) * 2 + c) for v in z_of]
    far = [at(x * 4 + d, y * 4 + (1 - zh) * 2 + c) for d in range(4)]
    targets = [at(lax.rem(me + d, PEERS), tile) for d in range(1, PEERS)]
    targets += [at(me, below), at(me, above), partner] + y_peer[1:] + far
    signal_all(pltpu.get_barrier_semaphore(), targets)

    core_copy = remote(probe.at[pl.ds(pl.multiple_of((1 - c) * 1024, 1024), 1024)], cbuf,
                       core_send.at[0], core_recv.at[0], partner)
    core_copy.start()

    def object_copy(d):
        q = lax.rem(me + d, PEERS)
        return remote(gp.at[q], gin.at[d], obj_send.at[d], obj_recv.at[d], at(q, tile))

    def start_object(d, carry):
        object_copy(d).start()
        return carry

    lax.fori_loop(1, PEERS, start_object, 0)
    gin[0] = gp[me]

    def scatter(src, buf, peer, index, size, send, recv, dest, own_size):
        copies = []
        for d in range(1, len(peer)):
            start = pl.multiple_of(index[d] * size, 8)
            copy = remote(src.at[pl.ds(start, size)], buf.at[d - 1], send.at[d], recv.at[d], peer[d])
            copy.start()
            copies.append(copy)
        for copy in copies:
            copy.wait()
        total = src[pl.ds(pl.multiple_of(index[0] * size, 8), size)]
        for d in range(1, len(peer)):
            total = total + buf[d - 1]
        dest[...] = total

    def spread(start, size, peer, send, recv, offset):
        copies = []
        part = gout.at[pl.ds(pl.multiple_of(start, 8), size)]
        for d in range(1, len(peer)):
            copy = remote(part, part, send.at[offset + d], recv.at[offset + d], peer[d])
            copy.start()
            copies.append(copy)
        for copy in copies:
            copy.wait()

    core_copy.wait()
    work[...] = probe[pl.ds(pl.multiple_of(c * 1024, 1024), 1024)] + cbuf[...]
    scatter(work, ybuf, y_peer, y_of, 256, y_send, y_recv, work2, 256)
    scatter(work2, xbuf, x_peer, x_of, 64, x_send, x_recv, work3, 64)
    base = c * 1024
    y_base = base + y * 256
    x_base = y_base + x * 64
    z_base = x_base + z * 8
    scatter(work3, zbuf, z_peer, z_of, 8, z_send, z_recv, gout.at[pl.ds(pl.multiple_of(z_base, 8), 8)], 8)
    spread(z_base, 8, z_peer, z_send, z_recv, 8)

    def finish_object(d, carry):
        object_copy(d).wait()
        return carry

    lax.fori_loop(1, PEERS, finish_object, 0)
    row = lax.broadcasted_iota(jnp.int32, (8, SIDE), 0) + me * 8
    lane = lax.broadcasted_iota(jnp.int32, (8, SIDE), 1)
    for ch in range(4):
        def add(d, acc):
            q = lax.rem(me + PEERS - d, PEERS)
            acc = list(acc)
            for j in range(SLOTS):
                a, block, shift = offset_of(offs, q, j)
                piece = pltpu.roll(gin[d, j * 32 + ch * 8:j * 32 + ch * 8 + 8], shift, 1)
                mine = jnp.where(row >= a, piece, 0.0)
                other = piece - mine
                target = jnp.where(lane < shift, block + 1, block)
                for k in range(8):
                    mask = target == k
                    acc[k] = acc[k] + jnp.where(mask, mine, 0.0)
                    acc[8 + k] = acc[8 + k] + jnp.where(mask, other, 0.0)
            return tuple(acc)

        zero = jnp.zeros((8, SIDE), f32)
        acc = lax.fori_loop(0, PEERS, add, (zero,) * 16)
        for k in range(8):
            out[ch * 8:ch * 8 + 8, k * SIDE:(k + 1) * SIDE] = acc[k]
            nacc[ch * 8:ch * 8 + 8, k * SIDE:(k + 1) * SIDE] = acc[8 + k]
    next_copy = remote(nacc, nin, nxt_send, nxt_recv, at(me, above))
    next_copy.start()
    spread(x_base, 64, x_peer, x_send, x_recv, 4)
    spread(y_base, 256, y_peer, y_send, y_recv, 4)
    half = gout.at[pl.ds(pl.multiple_of(base, 1024), 1024)]
    back_copy = remote(half, half, core_send.at[1], core_recv.at[1], partner)
    back_copy.start()
    next_copy.wait()
    out[...] += nin[...]
    back_copy.wait()


def reduce_all(offs, gp, probe):
    vm = pl.BlockSpec(memory_space=pltpu.VMEM)
    sm = pl.BlockSpec(memory_space=pltpu.SMEM)
    dma = pltpu.SemaphoreType.DMA
    return pl.pallas_call(
        reduce_kernel,
        out_shape=[
            jax.ShapeDtypeStruct((32, 1024), f32),
            jax.ShapeDtypeStruct((2048, SIDE), f32),
        ],
        in_specs=[sm, vm, vm],
        out_specs=[vm, vm],
        scratch_shapes=[
            pltpu.VMEM((PEERS, ROWS, SIDE), f32),
            pltpu.VMEM((32, 1024), f32),
            pltpu.VMEM((32, 1024), f32),
            pltpu.VMEM((1024, SIDE), f32),
            pltpu.VMEM((1024, SIDE), f32),
            pltpu.VMEM((3, 256, SIDE), f32),
            pltpu.VMEM((256, SIDE), f32),
            pltpu.VMEM((3, 64, SIDE), f32),
            pltpu.VMEM((64, SIDE), f32),
            pltpu.VMEM((7, 8, SIDE), f32),
            dma((PEERS,)), dma((PEERS,)), dma, dma, dma((2,)), dma((2,)),
            dma((8,)), dma((8,)), dma((8,)), dma((8,)), dma((16,)), dma((16,)),
        ],
        compiler_params=pltpu.CompilerParams(
            collective_id=1, has_side_effects=True, vmem_limit_bytes=32 << 20
        ),
        name="reduce_all",
    )(offs, gp, probe)


def tables(n):
    k=np.arange(n)
    f=np.exp(-2j*np.pi*(np.outer(k,k)%n)/n)/math.sqrt(n)
    fr=((k+n//2)%n-n//2)/n
    ph=np.exp(-1j*np.pi*24.0*fr**2)
    a=np.conj(f)@(ph[:,None]*f)
    out=[]
    for m in (a,f):
        right=np.block([[m.real,m.imag],[-m.imag,m.real]]).astype(np.float32)
        left=np.block([[m.real,-m.imag],[m.imag,m.real]]).astype(np.float32)
        for t in (right,left):
            hi=t.astype(ml_dtypes.bfloat16)
            lo=(t-hi.astype(np.float32)).astype(ml_dtypes.bfloat16)
            out.append(np.stack([hi,lo]))
    return np.stack(out)

def split(x):
    hi=x.astype(bf16)
    return hi,(x-hi.astype(f32)).astype(bf16)

def dot(a,b):
    return jnp.dot(a,b,preferred_element_type=f32)

def two_sided(tab,which,xr,xi,G):
    x=jnp.concatenate([jnp.concatenate([r,i],axis=1) for r,i in zip(xr,xi)],axis=0)
    h,l=split(x)
    wh,wl=tab[2*which,0],tab[2*which,1]
    z=dot(h,wh)+dot(l,wh)+dot(h,wl)
    P=128
    d=jnp.concatenate([jnp.concatenate([z[m*P:(m+1)*P,c*P:(c+1)*P] for m in range(G)],axis=1) for c in range(2)],axis=0)
    h,l=split(d)
    wh,wl=tab[2*which+1,0],tab[2*which+1,1]
    o=dot(wh,h)+dot(wh,l)+dot(wl,h)
    return [o[:P,m*P:(m+1)*P] for m in range(G)],[o[P:,m*P:(m+1)*P] for m in range(G)]

def kernel(G,M,S,offs,cnt,pieces,probe,pat,tab,gp,gprobe,dbl,win,phi,psi,inten):
    P=128
    for m in range(M):
        for c in range(2):
            gprobe[m,c]=jnp.zeros((P,P),f32)
    gp[...]=jnp.zeros(gp.shape,f32)
    def slot(j,_):
        a=offs[j,0]
        for ch in range(4):
            for p in range(16):
                start=pl.multiple_of(j*32+(ch//2)*16,16)
                v=pieces[p,pl.ds(start,16),:].astype(f32)[(ch%2)*8:(ch%2)*8+8]
                dbl[ch,p*8:p*8+8]=v
                dbl[ch,P+p*8:P+p*8+8]=v
        for ch in range(4):
            win[ch]=dbl[ch,pl.ds(a,P),:]
        inten[...]=-pat[j]
        def fwd(i,_):
            m0=i*G
            w0r,w0i=win[0],win[1]
            xr=[];xi=[]
            for g in range(G):
                pr,pi=probe[m0+g,0],probe[m0+g,1]
                xr.append(pr*w0r-pi*w0i); xi.append(pr*w0i+pi*w0r)
            zr,zi=two_sided(tab,0,xr,xi,G)
            w1r,w1i=win[2],win[3]
            xr=[];xi=[]
            for g in range(G):
                phi[m0+g,0]=zr[g]; phi[m0+g,1]=zi[g]
                xr.append(zr[g]*w1r-zi[g]*w1i); xi.append(zr[g]*w1i+zi[g]*w1r)
            zr,zi=two_sided(tab,1,xr,xi,G)
            acc=inten[...]
            for g in range(G):
                psi[m0+g,0]=zr[g]; psi[m0+g,1]=zi[g]
                acc=acc+zr[g]*zr[g]+zi[g]*zi[g]
            inten[...]=acc
            return 0
        lax.fori_loop(0,M//G,fwd,0)
        for ch in range(4):
            dbl[ch,:P]=jnp.zeros((P,P),f32)
        def bwd(i,_):
            m0=i*G
            res=2.0*inten[...]
            xr=[];xi=[]
            for g in range(G):
                xr.append(psi[m0+g,0]*res); xi.append(psi[m0+g,1]*-res)
            zr,zi=two_sided(tab,1,xr,xi,G)
            w1r,w1i=win[2],win[3]
            ar=dbl[2,:P]; ai=dbl[3,:P]
            xr=[];xi=[]
            for g in range(G):
                fr,fi=phi[m0+g,0],phi[m0+g,1]
                ar=ar+(fr*zr[g]-fi*zi[g]); ai=ai-(fr*zi[g]+fi*zr[g])
                xr.append(zr[g]*w1r-zi[g]*w1i); xi.append(zr[g]*w1i+zi[g]*w1r)
            dbl[2,:P]=ar; dbl[3,:P]=ai
            zr,zi=two_sided(tab,0,xr,xi,G)
            w0r,w0i=win[0],win[1]
            ar=dbl[0,:P]; ai=dbl[1,:P]
            for g in range(G):
                pr,pi=probe[m0+g,0],probe[m0+g,1]
                ar=ar+(pr*zr[g]-pi*zi[g]); ai=ai-(pr*zi[g]+pi*zr[g])
                gprobe[m0+g,0]+=zr[g]*w0r-zi[g]*w0i
                gprobe[m0+g,1]-=zr[g]*w0i+zi[g]*w0r
            dbl[0,:P]=ar; dbl[1,:P]=ai
            return 0
        lax.fori_loop(0,M//G,bwd,0)
        for ch in range(4):
            dbl[ch,P:]=dbl[ch,:P]
        for ch in range(4):
            r=dbl[ch,pl.ds(P-a,P),:]
            for p in range(16):
                start=pl.multiple_of(j*32+ch*8,8)
                gp[p,pl.ds(start,8),:]=r[p*8:p*8+8]
        return 0
    lax.fori_loop(0,cnt[0,0],slot,0)

def compute(offs,cnt,pieces,probe,pat,tab,G=2):
    M,S=probe.shape[0],pat.shape[0]
    sm=pl.BlockSpec(memory_space=pltpu.SMEM); vm=pl.BlockSpec(memory_space=pltpu.VMEM)
    return pl.pallas_call(functools.partial(kernel,G,M,S),
        out_shape=[jax.ShapeDtypeStruct((16,S*32,128),f32),jax.ShapeDtypeStruct(probe.shape,f32)],
        in_specs=[sm,sm,vm,vm,vm,vm],out_specs=[vm,vm],
        scratch_shapes=[pltpu.VMEM((4,256,128),f32),pltpu.VMEM((4,128,128),f32),
            pltpu.VMEM((M,2,128,128),f32),pltpu.VMEM((M,2,128,128),f32),pltpu.VMEM((128,128),f32)],
        compiler_params=pltpu.CompilerParams(vmem_limit_bytes=48<<20),name="ptycho")(offs,cnt,pieces,probe,pat,tab)


def per_device(object_slices, probe_modes, offsets, counts, patterns):
    shard = object_slices.reshape(32, 1024)
    off = jnp.pad(offsets.reshape(1, 2 * SLOTS), ((0, 0), (0, SIDE - 2 * SLOTS)))
    pieces, offs = gather_windows(off, shard)
    gp, gprobe = compute(offsets[0, 0], counts, pieces, probe_modes, patterns[0, 0], jnp.asarray(tables(SIDE)), 8)
    out, gout = reduce_all(offs, gp, gprobe.reshape(2048, SIDE))
    return out.reshape(object_slices.shape), gout.reshape(probe_modes.shape)


def solution(mesh):
    placed = (
        P("tile", None, None, "pos", None),
        P(),
        P("tile", "pos", None, None),
        P("tile", "pos"),
        P("tile", "pos", None, None, None),
    )
    return jax.shard_map(
        per_device,
        mesh=mesh,
        in_specs=placed,
        out_specs=(P("tile", None, None, "pos", None), P()),
        check_vma=False,
    )
```

time: 786 us -> 120 us (0.15); the launches traced: 772 us -> 119 us
  waiting for transfers between devices: 447 us -> 0 us
  matrix products: 156 us -> 0 us
  Pallas kernels: 0 us -> 111 us
  local copies, waits for them, and re-layouts: 78 us -> 6.81 us
  other arithmetic: 41.6 us -> 0 us
  loops' own time: 19.8 us -> 0 us
  starting transfers between devices: 14.6 us -> 0 us
  between operations: 14.8 us -> 1.32 us
    psum x1 -> x0, waiting for transfers between devices: 226 us -> none  [per_device(): probe_out = lax.psum(probe_grad, ('pos', 'tile'))]
    dot_general x96 -> x0, matrix products: 156 us -> none  [the longest x24 39.2 us: transform(): left_real = jnp.einsum('ij,mcjl->mcil', real_table, half, precision=highest)]
    pallas_call x0 -> x3, Pallas kernels: none -> 111 us  [the longest x1 70.4 us: reduce_all(): pl.pallas_call(reduce_kernel, out_shape=[jax.ShapeDtypeStruct((32, 1024),...]
    reduce_scatter x1 -> x0, waiting for transfers between devices: 84.8 us -> none  [per_device(): lax.psum_scatter(own_part + moved, 'pos', scatter_dimension=3, tiled=True)]
    all_gather x1 -> x0, waiting for transfers between devices: 78 us -> none  [per_device(): own_tile = lax.all_gather(object_slices, 'pos', axis=3, tiled=True)]
    ppermute x2 -> x0, waiting for transfers between devices: 57.8 us -> none  [from_behind(): return lax.ppermute(block, axis, route)]
    reduce_sum x16 -> x0, local copies, waits for them, and re-layouts: 25.1 us -> none  [the longest x8 12.6 us: multiply(): imag_part = field[:, 0] * factor[1] + field[:, 1] * factor[0]]
    dynamic_update_slice x8 -> x0, local copies, waits for them, and re-layouts: 20.7 us -> none  [add_position(): lax.dynamic_update_slice(object_grad, current + window_term, starts)]
  transfers between devices with their start and end apart: 5 -> 0, of which waited for: 5 -> 0; matrix products, arithmetic and copies ran while one was open for 1% -> 0% of each run, Pallas kernels for 0% -> 0%
where the time goes in v1:
time: 120 us; the launch traced here: 119 us
  Pallas kernels  111 us (92%)
  local copies, waits for them, and re-layouts  6.81 us (6%)
  between operations  1.32 us (1%)
    pallas_call x1, Pallas kernels, reduce_all(): pl.pallas_call(reduce_kernel, out_shape=[jax.ShapeDtypeStruct((32, 1024),...  70.4 us
    pallas_call x1, Pallas kernels, gather_windows(): pl.pallas_call(gather_kernel, out_shape=[jax.ShapeDtypeStruct((PEERS, ROW...  26.6 us
    pallas_call x1, Pallas kernels, compute(): pl.pallas_call(functools.partial(kernel, G, M, S), out_shape=[jax.ShapeDt...  14.3 us
    unnamed x13, local copies, waits for them, and re-layouts  6.63 us

profile of v1, /device:TPU:1, one launch (start us, length us, event | category | flops | bytes accessed | tf_op | source)
XLA Modules:
  0.0 119.4 jit_solution(80342904709344790)
XLA Ops:
  1.3 0.0 copy-start.4
  1.3 0.7 copy-done.4
  2.0 0.1 copy.11.offs
  2.0 0.1 copy.10
  2.1 0.1 reshape.19
  2.2 0.0 copy-start.3
  2.2 0.8 copy-done.3
  3.1 26.6 %gather_windows.1 = (bf16[16,128,128]{2,1,0:T(8,128)(2,1)S(1)}, s32[16,1,128]{2,1,0:T(1,128)S(1)}) custom-call(s32[1,128]{1,0:T(1,128)S(1)} %pad.4.off, bf16[32,1024]{1,0:T(8,128)(2,1)S(1)} %bitcast.10), custom_call_target="tpu_custom_call" | custom-call | tf_op jit(solution)/shard_map/gather_windows/pallas_call | solution.py:114
  29.7 0.0 copy-start
  29.7 1.2 %copy-done = f32[8,2,128,128]{3,2,1,0:T(8,128)S(1)} copy-done((f32[8,2,128,128]{3,2,1,0:T(8,128)S(1)}, f32[8,2,128,128]{3,2,1,0:T(8,128)}, u32[]{:S(2)}) %copy-start) | copy-done | bytes 1048600
  30.9 0.0 copy-start.1
  30.9 1.2 %copy-done.1 = bf16[4,2,256,256]{3,2,1,0:T(8,128)(2,1)S(1)} copy-done((bf16[4,2,256,256]{3,2,1,0:T(8,128)(2,1)S(1)}, bf16[4,2,256,256]{3,2,1,0:T(8,128)(2,1)}, u32[]{:S(2)}) %copy-start.1) | copy-done | bytes 1048600
  32.1 0.0 copy-start.2
  32.1 0.9 copy-done.2
  33.1 14.3 %ptycho.1 = (f32[16,128,128]{2,1,0:T(8,128)S(1)}, f32[8,2,128,128]{3,2,1,0:T(8,128)S(1)}) custom-call(s32[4,2]{1,0:T(4,128)S(1)} %copy.11.offs, s32[1,1]{1,0:T(1,128)S(6)} %copy.14.cnt, bf16[16,128,128]{2,1,0:T(8,128)(2,1)S(1)} %get-tuple-element.9.pieces, f32[8,2,128,128]{3,2,1,0:T(8,128)S(1)} %copy-done, f32[4,128,128]{2,1,0:T(8,128)S(1)} %bitcast.8, ...), custom_call_target="tpu_custom_call" | custom-call | tf_op jit(solution)/shard_map/ptycho/pallas_call | solution.py:396
  47.4 70.4 %reduce_all.1 = (f32[32,1024]{1,0:T(8,128)S(1)}, f32[2048,128]{1,0:T(8,128)S(1)}) custom-call(s32[16,1,128]{2,1,0:T(1,128)S(1)} %get-tuple-element.8.offs, f32[16,128,128]{2,1,0:T(8,128)S(1)} %get-tuple-element.10.gp, f32[2048,128]{1,0:T(8,128)S(1)} %bitcast.6), custom_call_target="tpu_custom_call" | custom-call | tf_op jit(solution)/shard_map/reduce_all/pallas_call | solution.py:253
  117.8 0.7 copy.15
  118.5 1.0 copy.16
  (1 shorter events, 0.0 us)
Async XLA Ops:
  1.3 0.7 copy-start.4
  2.2 0.8 copy-start.3
  29.7 1.2 %copy-start = (f32[8,2,128,128]{3,2,1,0:T(8,128)S(1)}, f32[8,2,128,128]{3,2,1,0:T(8,128)}, u32[]{:S(2)}) copy-start(f32[8,2,128,128]{3,2,1,0:T(8,128)} %probe.1) | copy-start | bytes 3145732
  30.9 1.2 %copy-start.1 = (bf16[4,2,256,256]{3,2,1,0:T(8,128)(2,1)S(1)}, bf16[4,2,256,256]{3,2,1,0:T(8,128)(2,1)}, u32[]{:S(2)}) copy-start(bf16[4,2,256,256]{3,2,1,0:T(8,128)(2,1)} %constant.4.clone.tab) | copy-start | bytes 3145732
  32.1 0.9 copy-start.2

commit v2 on v0

v2 whole, which is shorter than its diff:
```python
import functools
import math

import jax
import jax.numpy as jnp
import ml_dtypes
import numpy as np
from jax import lax
from jax.experimental import pallas as pl
from jax.experimental.pallas import tpu as pltpu
from jax.sharding import PartitionSpec as P

f32 = jnp.float32
bf16 = jnp.bfloat16
MESH = pl.DeviceIdType.MESH
SIDE = 128
PEERS = 16
SLOTS = 4
TILES = 16
MODES = 8


def signal_all(barrier, targets):
    for target in targets:
        pl.semaphore_signal(barrier, inc=1, device_id=target, device_id_type=MESH)
    pl.semaphore_wait(barrier, len(targets))


def remote(src, dst, send, recv, target):
    return pltpu.make_async_remote_copy(
        src_ref=src, dst_ref=dst, send_sem=send, recv_sem=recv,
        device_id=target, device_id_type=MESH,
    )


def at(pos, tile):
    return {"pos": pos, "tile": tile}


def offset_of(offs, q, j):
    a = offs[q, 0, 2 * j]
    b = offs[q, 0, 2 * j + 1]
    block = lax.div(b, SIDE)
    return a, block, b - block * SIDE


def tables(n):
    k=np.arange(n)
    f=np.exp(-2j*np.pi*(np.outer(k,k)%n)/n)/math.sqrt(n)
    fr=((k+n//2)%n-n//2)/n
    ph=np.exp(-1j*np.pi*24.0*fr**2)
    a=np.conj(f)@(ph[:,None]*f)
    out=[]
    for m in (a,f):
        right=np.block([[m.real,m.imag],[-m.imag,m.real]]).astype(np.float32)
        left=np.block([[m.real,-m.imag],[m.imag,m.real]]).astype(np.float32)
        for t in (right,left):
            hi=t.astype(ml_dtypes.bfloat16)
            lo=(t-hi.astype(np.float32)).astype(ml_dtypes.bfloat16)
            out.append(np.stack([hi,lo]))
    return np.stack(out)

def split(x):
    hi=x.astype(bf16)
    return hi,(x-hi.astype(f32)).astype(bf16)

def dot(a,b):
    return jnp.dot(a,b,preferred_element_type=f32)

def two_sided(tab,which,xr,xi,G):
    x=jnp.concatenate([jnp.concatenate([r,i],axis=1) for r,i in zip(xr,xi)],axis=0)
    h,l=split(x)
    wh,wl=tab[2*which,0],tab[2*which,1]
    z=dot(h,wh)+dot(l,wh)+dot(h,wl)
    P=128
    d=jnp.concatenate([jnp.concatenate([z[m*P:(m+1)*P,c*P:(c+1)*P] for m in range(G)],axis=1) for c in range(2)],axis=0)
    h,l=split(d)
    wh,wl=tab[2*which+1,0],tab[2*which+1,1]
    o=dot(wh,h)+dot(wh,l)+dot(wl,h)
    return [o[:P,m*P:(m+1)*P] for m in range(G)],[o[P:,m*P:(m+1)*P] for m in range(G)]


def fused_kernel(off, cnt, shard, probe_hbm, pat_hbm, tab_hbm, out, gout,
                 probe, pat, tab, nxt, own_f, nxt_f, wstage, pieces, offs_v, offs,
                 dbl, win, phi, psi, inten, gprobe, gp, gin, nacc, nin,
                 cbuf, work, xybuf, zbuf,
                 local_sem, off_send, off_recv, nxt_send, nxt_recv, win_send, win_recv,
                 obj_send, obj_recv, core_send, core_recv, xy_send, xy_recv, z_send, z_recv):
    me = lax.axis_index("pos")
    tile = lax.axis_index("tile")
    x, zl = lax.div(me, 4), lax.rem(me, 4)
    y, zh, c = lax.div(tile, 4), lax.rem(lax.div(tile, 2), 2), lax.rem(tile, 2)
    z = zh * 4 + zl
    index = y * 4 + x
    below = lax.rem(tile + TILES - 1, TILES)
    above = lax.rem(tile + 1, TILES)
    partner = at(me, tile + 1 - 2 * c)

    def xy_peer(d):
        px, py = lax.rem(x + lax.rem(d, 4), 4), lax.rem(y + lax.div(d, 4), 4)
        return py * 4 + px, at(px * 4 + zl, py * 4 + zh * 2 + c)

    def z_peer(d):
        pz = lax.rem(z + d, 8)
        return at(x * 4 + lax.rem(pz, 4), y * 4 + lax.div(pz, 4) * 2 + c)

    loads = [
        pltpu.make_async_copy(probe_hbm, probe, local_sem.at[0]),
        pltpu.make_async_copy(tab_hbm, tab, local_sem.at[1]),
        pltpu.make_async_copy(pat_hbm, pat, local_sem.at[2]),
    ]
    for load in loads:
        load.start()
    targets = [at(lax.rem(me + d, PEERS), tile) for d in range(1, PEERS)]
    targets += [xy_peer(d)[1] for d in range(4, PEERS)]
    targets += [at(x * 4 + d, y * 4 + (1 - zh) * 2 + c) for d in range(4)]
    targets += [at(me, below), at(me, above), partner]
    signal_all(pltpu.get_barrier_semaphore(), targets)

    first_next = remote(shard, nxt, nxt_send.at[0], nxt_recv.at[0], at(me, below))
    first_next.start()

    def off_copy(d):
        return remote(off, offs_v.at[me], off_send.at[d], off_recv.at[d], at(lax.rem(me + d, PEERS), tile))

    def each_peer(action):
        def step(d, carry):
            action(d)
            return carry

        lax.fori_loop(1, PEERS, step, 0)

    each_peer(lambda d: off_copy(d).start())
    offs_v[me] = off[...]
    for block in range(8):
        own_f[block] = shard[:, block * SIDE:(block + 1) * SIDE].astype(f32)
    own_f[8] = jnp.zeros((32, SIDE), f32)
    nxt_f[8] = jnp.zeros((32, SIDE), f32)
    gprobe[...] = jnp.zeros(gprobe.shape, f32)
    out[...] = jnp.zeros(out.shape, f32)
    nacc[...] = jnp.zeros(nacc.shape, f32)
    each_peer(lambda d: off_copy(d).wait())
    to_smem = pltpu.make_async_copy(offs_v, offs, local_sem.at[3])
    to_smem.start()
    first_next.wait()
    for block in range(8):
        nxt_f[block] = nxt[:, block * SIDE:(block + 1) * SIDE].astype(f32)
    to_smem.wait()

    row32 = lax.rem(lax.broadcasted_iota(jnp.int32, (32, SIDE), 0), 8) + me * 8
    lane32 = lax.broadcasted_iota(jnp.int32, (32, SIDE), 1)

    def cut(q, j):
        a, block, shift = offset_of(offs, q, j)
        mask = row32 >= a
        left = jnp.where(mask, own_f[block], nxt_f[block])
        right = jnp.where(mask, own_f[block + 1], nxt_f[block + 1])
        back = lax.rem(SIDE - shift, SIDE)
        both = jnp.where(lane32 < SIDE - shift, pltpu.roll(left, back, 1), pltpu.roll(right, back, 1))
        return both.astype(bf16)

    def window_copy(j, d):
        q = lax.rem(me + d, PEERS)
        return remote(wstage.at[j, q], pieces.at[j, me], win_send.at[j, d], win_recv.at[j, d], at(q, tile))

    def send_windows(j, carry):
        def send(d):
            q = lax.rem(me + d, PEERS)
            wstage[j, q] = cut(q, j)
            window_copy(j, d).start()

        each_peer(send)
        pieces[j, me] = cut(me, j)
        return carry

    lax.fori_loop(0, SLOTS, send_windows, 0)

    def object_copy(j, d):
        q = lax.rem(me + d, PEERS)
        return remote(gp.at[j, q], gin.at[j, d], obj_send.at[j, d], obj_recv.at[j, d], at(q, tile))

    for load in loads:
        load.wait()
    live_count = cnt[0, 0]

    def slot(j, carry):
        each_peer(lambda d: window_copy(j, d).wait())
        a = offs[me, 0, 2 * j]
        for p in range(PEERS):
            piece = pieces[j, p].astype(f32)
            for ch in range(4):
                part = piece[ch * 8:ch * 8 + 8]
                dbl[ch, p * 8:p * 8 + 8] = part
                dbl[ch, SIDE + p * 8:SIDE + p * 8 + 8] = part
        for ch in range(4):
            win[ch] = dbl[ch, pl.ds(a, SIDE), :]
        w0r, w0i = win[0], win[1]
        xr, xi = [], []
        for m in range(MODES):
            pr, pi = probe[m, 0], probe[m, 1]
            xr.append(pr * w0r - pi * w0i)
            xi.append(pr * w0i + pi * w0r)
        zr, zi = two_sided(tab, 0, xr, xi, MODES)
        w1r, w1i = win[2], win[3]
        xr, xi = [], []
        for m in range(MODES):
            phi[m, 0] = zr[m]
            phi[m, 1] = zi[m]
            xr.append(zr[m] * w1r - zi[m] * w1i)
            xi.append(zr[m] * w1i + zi[m] * w1r)
        zr, zi = two_sided(tab, 1, xr, xi, MODES)
        total = -pat[j]
        for m in range(MODES):
            psi[m, 0] = zr[m]
            psi[m, 1] = zi[m]
            total = total + zr[m] * zr[m] + zi[m] * zi[m]
        slot_number = jnp.zeros((SIDE, SIDE), jnp.int32) + j
        inten[...] = jnp.where(slot_number < live_count, 2.0 * total, 0.0)

        res = inten[...]
        xr, xi = [], []
        for m in range(MODES):
            xr.append(psi[m, 0] * res)
            xi.append(psi[m, 1] * -res)
        zr, zi = two_sided(tab, 1, xr, xi, MODES)
        w1r, w1i = win[2], win[3]
        ar = ai = jnp.zeros((SIDE, SIDE), f32)
        xr, xi = [], []
        for m in range(MODES):
            fr, fi = phi[m, 0], phi[m, 1]
            ar = ar + (fr * zr[m] - fi * zi[m])
            ai = ai - (fr * zi[m] + fi * zr[m])
            xr.append(zr[m] * w1r - zi[m] * w1i)
            xi.append(zr[m] * w1i + zi[m] * w1r)
        for half in range(2):
            dbl[2, half * SIDE:(half + 1) * SIDE] = ar
            dbl[3, half * SIDE:(half + 1) * SIDE] = ai
        zr, zi = two_sided(tab, 0, xr, xi, MODES)
        w0r, w0i = win[0], win[1]
        ar = ai = jnp.zeros((SIDE, SIDE), f32)
        for m in range(MODES):
            pr, pi = probe[m, 0], probe[m, 1]
            ar = ar + (pr * zr[m] - pi * zi[m])
            ai = ai - (pr * zi[m] + pi * zr[m])
            gprobe[8 * m:8 * m + 4] += (zr[m] * w0r - zi[m] * w0i).reshape(4, 32, SIDE)
            gprobe[8 * m + 4:8 * m + 8] -= (zr[m] * w0i + zi[m] * w0r).reshape(4, 32, SIDE)
        for half in range(2):
            dbl[0, half * SIDE:(half + 1) * SIDE] = ar
            dbl[1, half * SIDE:(half + 1) * SIDE] = ai
        for ch in range(4):
            rolled = dbl[ch, pl.ds(SIDE - a, SIDE), :]
            for p in range(PEERS):
                gp[j, p, ch * 8:ch * 8 + 8] = rolled[p * 8:p * 8 + 8]
        each_peer(lambda d: object_copy(j, d).start())
        gin[j, 0] = gp[j, me]
        return carry

    lax.fori_loop(0, SLOTS, slot, 0)

    def core_copy(k):
        src = gprobe.at[pl.ds(32 * k + 16 * (1 - c), 16)]
        return remote(src, cbuf.at[k], core_send.at[k], core_recv.at[k], partner)

    def xy_copy(k, d):
        i, peer = xy_peer(d)
        return remote(work.at[k, i], xybuf.at[k, d], xy_send.at[k, d], xy_recv.at[k, d], peer)

    def z_copy(k, d):
        part = zbuf.at[k, z]
        return remote(part, part, z_send.at[k, d], z_recv.at[k, d], z_peer(d))

    def xy_back(k, d):
        part = gout.at[32 * k + 16 * c + index]
        return remote(part, part, xy_send.at[2 + k, d], xy_recv.at[2 + k, d], xy_peer(d)[1])

    def core_back(k):
        part = gout.at[pl.ds(32 * k + 16 * c, 16)]
        return remote(part, part, core_send.at[2 + k], core_recv.at[2 + k], partner)

    row8 = lax.broadcasted_iota(jnp.int32, (8, SIDE), 0) + me * 8
    lane8 = lax.broadcasted_iota(jnp.int32, (8, SIDE), 1)

    def accumulate(slots):
        for ch in range(4):
            def add(d, acc):
                q = lax.rem(me + PEERS - d, PEERS)
                acc = list(acc)
                for j in slots:
                    a, block, shift = offset_of(offs, q, j)
                    piece = pltpu.roll(gin[j, d, ch * 8:ch * 8 + 8], shift, 1)
                    mine = jnp.where(row8 >= a, piece, 0.0)
                    other = piece - mine
                    target = jnp.where(lane8 < shift, block + 1, block)
                    for k in range(8):
                        mask = target == k
                        acc[k] = acc[k] + jnp.where(mask, mine, 0.0)
                        acc[8 + k] = acc[8 + k] + jnp.where(mask, other, 0.0)
                return tuple(acc)

            cols = [slice(k * SIDE, (k + 1) * SIDE) for k in range(8)]
            rows = slice(ch * 8, ch * 8 + 8)
            acc = [out[rows, s] for s in cols] + [nacc[rows, s] for s in cols]
            acc = lax.fori_loop(0, PEERS, add, tuple(acc))
            for k in range(8):
                out[rows, cols[k]] = acc[k]
                nacc[rows, cols[k]] = acc[8 + k]

    for k in range(2):
        core_copy(k).start()
    for k in range(2):
        core_copy(k).wait()
        work[k] = gprobe[pl.ds(32 * k + 16 * c, 16)] + cbuf[k]
        each_peer(lambda d: xy_copy(k, d).start())
    for j in range(SLOTS - 1):
        each_peer(lambda d: object_copy(j, d).wait())
    accumulate(range(SLOTS - 1))
    each_peer(lambda d: object_copy(SLOTS - 1, d).wait())
    accumulate(range(SLOTS - 1, SLOTS))
    last_next = remote(nacc, nin, nxt_send.at[1], nxt_recv.at[1], at(me, above))
    last_next.start()
    for k in range(2):
        each_peer(lambda d: xy_copy(k, d).wait())
        total = work[k, index]
        for d in range(1, PEERS):
            total = total + xybuf[k, d]
        zbuf[k, z] = total
        for d in range(1, 8):
            z_copy(k, d).start()
    for k in range(2):
        for d in range(1, 8):
            z_copy(k, d).wait()
        total = zbuf[k, 0]
        for d in range(1, 8):
            total = total + zbuf[k, d]
        gout[32 * k + 16 * c + index] = total
        each_peer(lambda d: xy_back(k, d).start())
    for k in range(2):
        each_peer(lambda d: xy_back(k, d).wait())
        core_back(k).start()
    last_next.wait()
    out[...] += nin[...]
    for k in range(2):
        core_back(k).wait()


def fused(off, cnt, shard, probe, pat, tab):
    vm = pl.BlockSpec(memory_space=pltpu.VMEM)
    sm = pl.BlockSpec(memory_space=pltpu.SMEM)
    hbm = pl.BlockSpec(memory_space=pl.ANY)
    dma = pltpu.SemaphoreType.DMA
    vmem = pltpu.VMEM
    return pl.pallas_call(
        fused_kernel,
        out_shape=[
            jax.ShapeDtypeStruct((32, 1024), f32),
            jax.ShapeDtypeStruct((64, 32, SIDE), f32),
        ],
        in_specs=[vm, sm, vm, hbm, hbm, hbm],
        out_specs=[vm, vm],
        scratch_shapes=[
            vmem((MODES, 2, SIDE, SIDE), f32),
            vmem((SLOTS, SIDE, SIDE), f32),
            vmem((4, 2, 256, 256), bf16),
            vmem((32, 1024), bf16),
            vmem((9, 32, SIDE), f32),
            vmem((9, 32, SIDE), f32),
            vmem((SLOTS, PEERS, 32, SIDE), bf16),
            vmem((SLOTS, PEERS, 32, SIDE), bf16),
            vmem((PEERS, 1, SIDE), jnp.int32),
            pltpu.SMEM((PEERS, 1, SIDE), jnp.int32),
            vmem((4, 256, SIDE), f32),
            vmem((4, SIDE, SIDE), f32),
            vmem((MODES, 2, SIDE, SIDE), f32),
            vmem((MODES, 2, SIDE, SIDE), f32),
            vmem((SIDE, SIDE), f32),
            vmem((64, 32, SIDE), f32),
            vmem((SLOTS, PEERS, 32, SIDE), f32),
            vmem((SLOTS, PEERS, 32, SIDE), f32),
            vmem((32, 1024), f32),
            vmem((32, 1024), f32),
            vmem((2, 16, 32, SIDE), f32),
            vmem((2, 16, 32, SIDE), f32),
            vmem((2, 16, 32, SIDE), f32),
            vmem((2, 8, 32, SIDE), f32),
            dma((4,)), dma((PEERS,)), dma((PEERS,)), dma((2,)), dma((2,)),
            dma((SLOTS, PEERS)), dma((SLOTS, PEERS)), dma((SLOTS, PEERS)), dma((SLOTS, PEERS)),
            dma((4,)), dma((4,)), dma((4, PEERS)), dma((4, PEERS)), dma((2, 8)), dma((2, 8)),
        ],
        compiler_params=pltpu.CompilerParams(
            collective_id=0, has_side_effects=True, vmem_limit_bytes=48 << 20
        ),
        name="ptychography",
    )(off, cnt, shard, probe, pat, tab)


def per_device(object_slices, probe_modes, offsets, counts, patterns):
    shard = object_slices.reshape(32, 1024)
    off = jnp.pad(offsets.reshape(1, 2 * SLOTS), ((0, 0), (0, SIDE - 2 * SLOTS)))
    out, gout = fused(off, counts, shard, probe_modes, patterns[0, 0], jnp.asarray(tables(SIDE)))
    return out.reshape(object_slices.shape), gout.reshape(probe_modes.shape)


def solution(mesh):
    placed = (
        P("tile", None, None, "pos", None),
        P(),
        P("tile", "pos", None, None),
        P("tile", "pos"),
        P("tile", "pos", None, None, None),
    )
    return jax.shard_map(
        per_device,
        mesh=mesh,
        in_specs=placed,
        out_specs=(P("tile", None, None, "pos", None), P()),
        check_vma=False,
    )
```

time: 786 us -> 98.3 us (0.13); the launches traced: 772 us -> 98.1 us
  waiting for transfers between devices: 447 us -> 0 us
  matrix products: 156 us -> 0 us
  Pallas kernels: 0 us -> 90 us
  local copies, waits for them, and re-layouts: 78 us -> 6.72 us
  other arithmetic: 41.6 us -> 0 us
  loops' own time: 19.8 us -> 0 us
  starting transfers between devices: 14.6 us -> 0 us
  between operations: 14.8 us -> 1.3 us
    psum x1 -> x0, waiting for transfers between devices: 226 us -> none  [per_device(): probe_out = lax.psum(probe_grad, ('pos', 'tile'))]
    dot_general x96 -> x0, matrix products: 156 us -> none  [the longest x24 39.2 us: transform(): left_real = jnp.einsum('ij,mcjl->mcil', real_table, half, precision=highest)]
    pallas_call x0 -> x1, Pallas kernels: none -> 90 us  [fused(): pl.pallas_call(fused_kernel, out_shape=[jax.ShapeDtypeStruct((32, 1024),...]
    reduce_scatter x1 -> x0, waiting for transfers between devices: 84.8 us -> none  [per_device(): lax.psum_scatter(own_part + moved, 'pos', scatter_dimension=3, tiled=True)]
    all_gather x1 -> x0, waiting for transfers between devices: 78 us -> none  [per_device(): own_tile = lax.all_gather(object_slices, 'pos', axis=3, tiled=True)]
    ppermute x2 -> x0, waiting for transfers between devices: 57.8 us -> none  [from_behind(): return lax.ppermute(block, axis, route)]
    reduce_sum x16 -> x0, local copies, waits for them, and re-layouts: 25.1 us -> none  [the longest x8 12.6 us: multiply(): imag_part = field[:, 0] * factor[1] + field[:, 1] * factor[0]]
    dynamic_update_slice x8 -> x0, local copies, waits for them, and re-layouts: 20.7 us -> none  [add_position(): lax.dynamic_update_slice(object_grad, current + window_term, starts)]
  transfers between devices with their start and end apart: 5 -> 0, of which waited for: 5 -> 0; matrix products, arithmetic and copies ran while one was open for 1% -> 0% of each run, Pallas kernels for 0% -> 0%
where the time goes in v2:
time: 98.3 us; the launch traced here: 98.1 us
  Pallas kernels  90 us (92%)
  local copies, waits for them, and re-layouts  6.72 us (7%)
  between operations  1.3 us (1%)
    pallas_call x1, Pallas kernels, fused(): pl.pallas_call(fused_kernel, out_shape=[jax.ShapeDtypeStruct((32, 1024),...  90 us
    unnamed x13, local copies, waits for them, and re-layouts  6.63 us

profile of v2, /device:TPU:1, one launch (start us, length us, event | category | flops | bytes accessed | tf_op | source)
XLA Modules:
  0.0 98.1 jit_solution(13140553200173038894)
XLA Ops:
  1.3 0.0 copy-start.4
  1.3 0.7 copy-done.4
  2.0 0.1 copy.9
  2.0 0.1 reshape.16
  2.1 0.0 copy-start
  2.1 1.2 %copy-done = f32[8,2,128,128]{3,2,1,0:T(8,128)S(1)} copy-done((f32[8,2,128,128]{3,2,1,0:T(8,128)S(1)}, f32[8,2,128,128]{3,2,1,0:T(8,128)}, u32[]{:S(2)}) %copy-start) | copy-done | bytes 1048600
  3.4 0.0 copy-start.1
  3.4 1.2 %copy-done.1 = bf16[4,2,256,256]{3,2,1,0:T(8,128)(2,1)S(1)} copy-done((bf16[4,2,256,256]{3,2,1,0:T(8,128)(2,1)S(1)}, bf16[4,2,256,256]{3,2,1,0:T(8,128)(2,1)}, u32[]{:S(2)}) %copy-start.1) | copy-done | bytes 1048600
  4.6 0.0 copy-start.2
  4.6 0.9 copy-done.2
  5.5 0.0 copy-start.3
  5.5 0.8 copy-done.3
  6.4 90.0 %ptychography.1 = (f32[32,1024]{1,0:T(8,128)S(1)}, f32[64,32,128]{2,1,0:T(8,128)S(1)}) custom-call(s32[1,128]{1,0:T(1,128)S(1)} %pad.4.off, s32[1,1]{1,0:T(1,128)S(6)} %copy.12.cnt, bf16[32,1024]{1,0:T(8,128)(2,1)S(1)} %bitcast.7, f32[8,2,128,128]{3,2,1,0:T(8,128)S(1)} %copy-done, f32[4,128,128]{2,1,0:T(8,128)S(1)} %bitcast.5, ...), custom_call_target="tpu_custom_call" | custom-call | tf_op jit(solution)/shard_map/ptychography/pallas_call | solution.py:352
  96.4 0.7 copy.13
  97.1 1.0 copy.14
  (1 shorter events, 0.0 us)
Async XLA Ops:
  1.3 0.7 copy-start.4
  2.1 1.2 %copy-start = (f32[8,2,128,128]{3,2,1,0:T(8,128)S(1)}, f32[8,2,128,128]{3,2,1,0:T(8,128)}, u32[]{:S(2)}) copy-start(f32[8,2,128,128]{3,2,1,0:T(8,128)} %probe_hbm.1) | copy-start | bytes 3145732
  3.4 1.2 %copy-start.1 = (bf16[4,2,256,256]{3,2,1,0:T(8,128)(2,1)S(1)}, bf16[4,2,256,256]{3,2,1,0:T(8,128)(2,1)}, u32[]{:S(2)}) copy-start(bf16[4,2,256,256]{3,2,1,0:T(8,128)(2,1)} %constant.4.clone.tab_hbm) | copy-start | bytes 3145732
  4.6 0.9 copy-start.2
  5.5 0.8 copy-start.3

commit v3 on v2

--- a/solution.py
+++ b/solution.py
@@ -67,21 +67,29 @@
 def dot(a,b):
     return jnp.dot(a,b,preferred_element_type=f32)
 
-def two_sided(tab,which,xr,xi,G):
-    x=jnp.concatenate([jnp.concatenate([r,i],axis=1) for r,i in zip(xr,xi)],axis=0)
-    h,l=split(x)
-    wh,wl=tab[2*which,0],tab[2*which,1]
-    z=dot(h,wh)+dot(l,wh)+dot(h,wl)
-    P=128
-    d=jnp.concatenate([jnp.concatenate([z[m*P:(m+1)*P,c*P:(c+1)*P] for m in range(G)],axis=1) for c in range(2)],axis=0)
-    h,l=split(d)
-    wh,wl=tab[2*which+1,0],tab[2*which+1,1]
-    o=dot(wh,h)+dot(wh,l)+dot(wl,h)
-    return [o[:P,m*P:(m+1)*P] for m in range(G)],[o[P:,m*P:(m+1)*P] for m in range(G)]
-
-
-def fused_kernel(off, cnt, shard, probe_hbm, pat_hbm, tab_hbm, out, gout,
-                 probe, pat, tab, nxt, own_f, nxt_f, wstage, pieces, offs_v, offs,
+
+def two_sided(tab, which, xr, xi):
+    right_hi, right_lo = tab[2 * which, 0], tab[2 * which, 1]
+    left_hi, left_lo = tab[2 * which + 1, 0], tab[2 * which + 1, 1]
+    halves = []
+    for m in range(0, MODES, 2):
+        rows = [jnp.concatenate([xr[i], xi[i]], axis=1) for i in (m, m + 1)]
+        hi, lo = split(jnp.concatenate(rows, axis=0))
+        z = dot(hi, right_hi) + dot(lo, right_hi) + dot(hi, right_lo)
+        top = jnp.concatenate([z[:SIDE, :SIDE], z[SIDE:, :SIDE]], axis=1)
+        bottom = jnp.concatenate([z[:SIDE, SIDE:], z[SIDE:, SIDE:]], axis=1)
+        halves.append(jnp.concatenate([top, bottom], axis=0))
+    real, imag = [], []
+    for half in halves:
+        hi, lo = split(half)
+        o = dot(left_hi, hi) + dot(left_hi, lo) + dot(left_lo, hi)
+        real += [o[:SIDE, :SIDE], o[:SIDE, SIDE:]]
+        imag += [o[SIDE:, :SIDE], o[SIDE:, SIDE:]]
+    return real, imag
+
+
+def fused_kernel(off_in, cnt, shard, probe_hbm, pat_hbm, tab_hbm, out, gout,
+                 off, probe, pat, tab, nxt, own_f, nxt_f, wstage, pieces, offs_v, offs,
                  dbl, win, phi, psi, inten, gprobe, gp, gin, nacc, nin,
                  cbuf, work, xybuf, zbuf,
                  local_sem, off_send, off_recv, nxt_send, nxt_recv, win_send, win_recv,
@@ -111,6 +119,13 @@
     ]
     for load in loads:
         load.start()
+    lane1 = lax.broadcasted_iota(jnp.int32, (1, SIDE), 1)
+    row = jnp.zeros((1, SIDE), jnp.int32)
+    for j in range(SLOTS):
+        for i in range(2):
+            row = jnp.where(lane1 == 2 * j + i, off_in[i, j], row)
+    off[...] = row
+    offs_v[me] = row
     targets = [at(lax.rem(me + d, PEERS), tile) for d in range(1, PEERS)]
     targets += [xy_peer(d)[1] for d in range(4, PEERS)]
     targets += [at(x * 4 + d, y * 4 + (1 - zh) * 2 + c) for d in range(4)]
@@ -131,7 +146,6 @@
         lax.fori_loop(1, PEERS, step, 0)
 
     each_peer(lambda d: off_copy(d).start())
-    offs_v[me] = off[...]
     for block in range(8):
         own_f[block] = shard[:, block * SIDE:(block + 1) * SIDE].astype(f32)
     own_f[8] = jnp.zeros((32, SIDE), f32)
@@ -200,7 +214,7 @@
             pr, pi = probe[m, 0], probe[m, 1]
             xr.append(pr * w0r - pi * w0i)
             xi.append(pr * w0i + pi * w0r)
-        zr, zi = two_sided(tab, 0, xr, xi, MODES)
+        zr, zi = two_sided(tab, 0, xr, xi)
         w1r, w1i = win[2], win[3]
         xr, xi = [], []
         for m in range(MODES):
@@ -208,7 +222,7 @@
             phi[m, 1] = zi[m]
             xr.append(zr[m] * w1r - zi[m] * w1i)
             xi.append(zr[m] * w1i + zi[m] * w1r)
-        zr, zi = two_sided(tab, 1, xr, xi, MODES)
+        zr, zi = two_sided(tab, 1, xr, xi)
         total = -pat[j]
         for m in range(MODES):
             psi[m, 0] = zr[m]
@@ -222,7 +236,7 @@
         for m in range(MODES):
             xr.append(psi[m, 0] * res)
             xi.append(psi[m, 1] * -res)
-        zr, zi = two_sided(tab, 1, xr, xi, MODES)
+        zr, zi = two_sided(tab, 1, xr, xi)
         w1r, w1i = win[2], win[3]
         ar = ai = jnp.zeros((SIDE, SIDE), f32)
         xr, xi = [], []
@@ -235,7 +249,7 @@
         for half in range(2):
             dbl[2, half * SIDE:(half + 1) * SIDE] = ar
             dbl[3, half * SIDE:(half + 1) * SIDE] = ai
-        zr, zi = two_sided(tab, 0, xr, xi, MODES)
+        zr, zi = two_sided(tab, 0, xr, xi)
         w0r, w0i = win[0], win[1]
         ar = ai = jnp.zeros((SIDE, SIDE), f32)
         for m in range(MODES):
@@ -311,6 +325,14 @@
         core_copy(k).wait()
         work[k] = gprobe[pl.ds(32 * k + 16 * c, 16)] + cbuf[k]
         each_peer(lambda d: xy_copy(k, d).start())
+    for k in range(2):
+        each_peer(lambda d: xy_copy(k, d).wait())
+        total = work[k, index]
+        for d in range(1, PEERS):
+            total = total + xybuf[k, d]
+        zbuf[k, z] = total
+        for d in range(1, 8):
+            z_copy(k, d).start()
     for j in range(SLOTS - 1):
         each_peer(lambda d: object_copy(j, d).wait())
     accumulate(range(SLOTS - 1))
@@ -319,14 +341,6 @@
     last_next = remote(nacc, nin, nxt_send.at[1], nxt_recv.at[1], at(me, above))
     last_next.start()
     for k in range(2):
-        each_peer(lambda d: xy_copy(k, d).wait())
-        total = work[k, index]
-        for d in range(1, PEERS):
-            total = total + xybuf[k, d]
-        zbuf[k, z] = total
-        for d in range(1, 8):
-            z_copy(k, d).start()
-    for k in range(2):
         for d in range(1, 8):
             z_copy(k, d).wait()
         total = zbuf[k, 0]
@@ -343,10 +357,10 @@
         core_back(k).wait()
 
 
-def fused(off, cnt, shard, probe, pat, tab):
+def fused(offsets, cnt, shard, probe, pat, tab):
     vm = pl.BlockSpec(memory_space=pltpu.VMEM)
     sm = pl.BlockSpec(memory_space=pltpu.SMEM)
-    hbm = pl.BlockSpec(memory_space=pl.ANY)
+    hbm = pl.BlockSpec(memory_space=pltpu.HBM)
     dma = pltpu.SemaphoreType.DMA
     vmem = pltpu.VMEM
     return pl.pallas_call(
@@ -355,9 +369,10 @@
             jax.ShapeDtypeStruct((32, 1024), f32),
             jax.ShapeDtypeStruct((64, 32, SIDE), f32),
         ],
-        in_specs=[vm, sm, vm, hbm, hbm, hbm],
+        in_specs=[sm, sm, vm, hbm, hbm, hbm],
         out_specs=[vm, vm],
         scratch_shapes=[
+            vmem((1, SIDE), jnp.int32),
             vmem((MODES, 2, SIDE, SIDE), f32),
             vmem((SLOTS, SIDE, SIDE), f32),
             vmem((4, 2, 256, 256), bf16),
@@ -387,16 +402,15 @@
             dma((4,)), dma((4,)), dma((4, PEERS)), dma((4, PEERS)), dma((2, 8)), dma((2, 8)),
         ],
         compiler_params=pltpu.CompilerParams(
-            collective_id=0, has_side_effects=True, vmem_limit_bytes=48 << 20
+            collective_id=0, has_side_effects=True, vmem_limit_bytes=53 << 20
         ),
         name="ptychography",
-    )(off, cnt, shard, probe, pat, tab)
+    )(offsets, cnt, shard, probe, pat, tab)
 
 
 def per_device(object_slices, probe_modes, offsets, counts, patterns):
     shard = object_slices.reshape(32, 1024)
-    off = jnp.pad(offsets.reshape(1, 2 * SLOTS), ((0, 0), (0, SIDE - 2 * SLOTS)))
-    out, gout = fused(off, counts, shard, probe_modes, patterns[0, 0], jnp.asarray(tables(SIDE)))
+    out, gout = fused(offsets.reshape(SLOTS, 2).T, counts, shard, probe_modes, patterns[0, 0], jnp.asarray(tables(SIDE)))
     return out.reshape(object_slices.shape), gout.reshape(probe_modes.shape)
 
 

time: 98.3 us -> 90 us (0.916)
  Pallas kernels: 90 us -> 83.1 us
  local copies, waits for them, and re-layouts: 6.72 us -> 5.41 us
    pallas_call x1, Pallas kernels: 90 us -> 83.1 us  [fused(): pl.pallas_call(fused_kernel, out_shape=[jax.ShapeDtypeStruct((32, 1024),...]
    unnamed x13 -> x8, local copies, waits for them, and re-layouts: 6.63 us -> 5.41 us
where the time goes in v3:
time: 90 us; the launch traced here: 89.8 us
  Pallas kernels  83.1 us (92%)
  local copies, waits for them, and re-layouts  5.41 us (6%)
  between operations  1.3 us (1%)
    pallas_call x1, Pallas kernels, fused(): pl.pallas_call(fused_kernel, out_shape=[jax.ShapeDtypeStruct((32, 1024),...  83.1 us
    unnamed x8, local copies, waits for them, and re-layouts  5.41 us

profile of v3, /device:TPU:1, one launch (start us, length us, event | category | flops | bytes accessed | tf_op | source)
XLA Modules:
  0.0 89.8 jit_solution(13922114562789003821)
XLA Ops:
  1.3 0.0 copy-start.2
  1.3 0.7 copy-done.2
  2.0 0.0 copy-start
  2.0 0.9 %copy-done = f32[1,1,4,128,128]{4,3,2,1,0:T(8,128)S(1)} copy-done((f32[1,1,4,128,128]{4,3,2,1,0:T(8,128)S(1)}, f32[1,1,4,128,128]{4,3,2,1,0:T(8,128)}, u32[]{:S(2)}) %copy-start) | copy-done | bytes 262168
  2.9 0.0 copy-start.1
  2.9 0.8 copy-done.1
  3.7 83.1 %ptychography.1 = (f32[32,1024]{1,0:T(8,128)S(1)}, f32[64,32,128]{2,1,0:T(8,128)}) custom-call(s32[2,4]{1,0:T(2,128)S(1)} %bitcast.10, s32[1,1]{1,0:T(1,128)S(6)} %copy.10.cnt, bf16[32,1024]{1,0:T(8,128)(2,1)S(1)} %bitcast.9, f32[8,2,128,128]{3,2,1,0:T(8,128)} %probe_hbm.1, f32[4,128,128]{2,1,0:T(8,128)S(1)} %bitcast.7, ...), custom_call_target="tpu_custom_call" | custom-call | tf_op jit(solution)/shard_map/ptychography/pallas_call | solution.py:366
  86.9 0.7 copy.11
  87.5 2.3 %copy.12 = f32[8,2,128,128]{3,2,1,0:T(8,128)} copy(f32[8,2,128,128]{3,2,1,0:T(8,128)} %bitcast.11) | data formatting | bytes 2097152
Async XLA Ops:
  1.3 0.7 copy-start.2
  2.0 0.9 %copy-start = (f32[1,1,4,128,128]{4,3,2,1,0:T(8,128)S(1)}, f32[1,1,4,128,128]{4,3,2,1,0:T(8,128)}, u32[]{:S(2)}) copy-start(f32[1,1,4,128,128]{4,3,2,1,0:T(8,128)} %param.10) | copy-start | bytes 786436
  2.9 0.8 copy-start.1

commit v4 on v3

--- a/solution.py
+++ b/solution.py
@@ -18,6 +18,9 @@
 SLOTS = 4
 TILES = 16
 MODES = 8
+CHUNKS = 2
+UNIT = 64 // CHUNKS
+PARTS = SIDE // UNIT
 
 
 def signal_all(barrier, targets):
@@ -169,9 +172,7 @@
         mask = row32 >= a
         left = jnp.where(mask, own_f[block], nxt_f[block])
         right = jnp.where(mask, own_f[block + 1], nxt_f[block + 1])
-        back = lax.rem(SIDE - shift, SIDE)
-        both = jnp.where(lane32 < SIDE - shift, pltpu.roll(left, back, 1), pltpu.roll(right, back, 1))
-        return both.astype(bf16)
+        return jnp.where(lane32 >= shift, left, right).astype(bf16)
 
     def window_copy(j, d):
         q = lax.rem(me + d, PEERS)
@@ -199,7 +200,7 @@
 
     def slot(j, carry):
         each_peer(lambda d: window_copy(j, d).wait())
-        a = offs[me, 0, 2 * j]
+        a, block, shift = offset_of(offs, me, j)
         for p in range(PEERS):
             piece = pieces[j, p].astype(f32)
             for ch in range(4):
@@ -207,7 +208,7 @@
                 dbl[ch, p * 8:p * 8 + 8] = part
                 dbl[ch, SIDE + p * 8:SIDE + p * 8 + 8] = part
         for ch in range(4):
-            win[ch] = dbl[ch, pl.ds(a, SIDE), :]
+            win[ch] = pltpu.roll(dbl[ch, pl.ds(a, SIDE), :], lax.rem(SIDE - shift, SIDE), 1)
         w0r, w0i = win[0], win[1]
         xr, xi = [], []
         for m in range(MODES):
@@ -256,13 +257,13 @@
             pr, pi = probe[m, 0], probe[m, 1]
             ar = ar + (pr * zr[m] - pi * zi[m])
             ai = ai - (pr * zi[m] + pi * zr[m])
-            gprobe[8 * m:8 * m + 4] += (zr[m] * w0r - zi[m] * w0i).reshape(4, 32, SIDE)
-            gprobe[8 * m + 4:8 * m + 8] -= (zr[m] * w0i + zi[m] * w0r).reshape(4, 32, SIDE)
+            gprobe[2 * m * PARTS:(2 * m + 1) * PARTS] += (zr[m] * w0r - zi[m] * w0i).reshape(PARTS, UNIT, SIDE)
+            gprobe[(2 * m + 1) * PARTS:(2 * m + 2) * PARTS] -= (zr[m] * w0i + zi[m] * w0r).reshape(PARTS, UNIT, SIDE)
         for half in range(2):
             dbl[0, half * SIDE:(half + 1) * SIDE] = ar
             dbl[1, half * SIDE:(half + 1) * SIDE] = ai
         for ch in range(4):
-            rolled = dbl[ch, pl.ds(SIDE - a, SIDE), :]
+            rolled = pltpu.roll(dbl[ch, pl.ds(SIDE - a, SIDE), :], shift, 1)
             for p in range(PEERS):
                 gp[j, p, ch * 8:ch * 8 + 8] = rolled[p * 8:p * 8 + 8]
         each_peer(lambda d: object_copy(j, d).start())
@@ -285,47 +286,50 @@
 
     def xy_back(k, d):
         part = gout.at[32 * k + 16 * c + index]
-        return remote(part, part, xy_send.at[2 + k, d], xy_recv.at[2 + k, d], xy_peer(d)[1])
+        return remote(part, part, xy_send.at[CHUNKS + k, d], xy_recv.at[CHUNKS + k, d], xy_peer(d)[1])
 
     def core_back(k):
         part = gout.at[pl.ds(32 * k + 16 * c, 16)]
-        return remote(part, part, core_send.at[2 + k], core_recv.at[2 + k], partner)
+        return remote(part, part, core_send.at[CHUNKS + k], core_recv.at[CHUNKS + k], partner)
 
     row8 = lax.broadcasted_iota(jnp.int32, (8, SIDE), 0) + me * 8
     lane8 = lax.broadcasted_iota(jnp.int32, (8, SIDE), 1)
 
     def accumulate(slots):
+        group = 4
         for ch in range(4):
-            def add(d, acc):
-                q = lax.rem(me + PEERS - d, PEERS)
+            def add(i, acc):
                 acc = list(acc)
-                for j in slots:
-                    a, block, shift = offset_of(offs, q, j)
-                    piece = pltpu.roll(gin[j, d, ch * 8:ch * 8 + 8], shift, 1)
-                    mine = jnp.where(row8 >= a, piece, 0.0)
-                    other = piece - mine
-                    target = jnp.where(lane8 < shift, block + 1, block)
-                    for k in range(8):
-                        mask = target == k
-                        acc[k] = acc[k] + jnp.where(mask, mine, 0.0)
-                        acc[8 + k] = acc[8 + k] + jnp.where(mask, other, 0.0)
+                for e in range(group):
+                    d = i * group + e
+                    q = lax.rem(me + PEERS - d, PEERS)
+                    for j in slots:
+                        a, block, shift = offset_of(offs, q, j)
+                        piece = gin[j, d, ch * 8:ch * 8 + 8]
+                        mine = jnp.where(row8 >= a, piece, 0.0)
+                        other = piece - mine
+                        target = jnp.where(lane8 < shift, block + 1, block)
+                        for k in range(8):
+                            mask = target == k
+                            acc[k] = acc[k] + jnp.where(mask, mine, 0.0)
+                            acc[8 + k] = acc[8 + k] + jnp.where(mask, other, 0.0)
                 return tuple(acc)
 
             cols = [slice(k * SIDE, (k + 1) * SIDE) for k in range(8)]
             rows = slice(ch * 8, ch * 8 + 8)
             acc = [out[rows, s] for s in cols] + [nacc[rows, s] for s in cols]
-            acc = lax.fori_loop(0, PEERS, add, tuple(acc))
+            acc = lax.fori_loop(0, PEERS // group, add, tuple(acc))
             for k in range(8):
                 out[rows, cols[k]] = acc[k]
                 nacc[rows, cols[k]] = acc[8 + k]
 
-    for k in range(2):
+    for k in range(CHUNKS):
         core_copy(k).start()
-    for k in range(2):
+    for k in range(CHUNKS):
         core_copy(k).wait()
         work[k] = gprobe[pl.ds(32 * k + 16 * c, 16)] + cbuf[k]
         each_peer(lambda d: xy_copy(k, d).start())
-    for k in range(2):
+    for k in range(CHUNKS):
         each_peer(lambda d: xy_copy(k, d).wait())
         total = work[k, index]
         for d in range(1, PEERS):
@@ -340,7 +344,7 @@
     accumulate(range(SLOTS - 1, SLOTS))
     last_next = remote(nacc, nin, nxt_send.at[1], nxt_recv.at[1], at(me, above))
     last_next.start()
-    for k in range(2):
+    for k in range(CHUNKS):
         for d in range(1, 8):
             z_copy(k, d).wait()
         total = zbuf[k, 0]
@@ -348,12 +352,12 @@
             total = total + zbuf[k, d]
         gout[32 * k + 16 * c + index] = total
         each_peer(lambda d: xy_back(k, d).start())
-    for k in range(2):
+    for k in range(CHUNKS):
         each_peer(lambda d: xy_back(k, d).wait())
         core_back(k).start()
     last_next.wait()
     out[...] += nin[...]
-    for k in range(2):
+    for k in range(CHUNKS):
         core_back(k).wait()
 
 
@@ -367,7 +371,7 @@
         fused_kernel,
         out_shape=[
             jax.ShapeDtypeStruct((32, 1024), f32),
-            jax.ShapeDtypeStruct((64, 32, SIDE), f32),
+            jax.ShapeDtypeStruct((32 * CHUNKS, UNIT, SIDE), f32),
         ],
         in_specs=[sm, sm, vm, hbm, hbm, hbm],
         out_specs=[vm, vm],
@@ -388,18 +392,19 @@
             vmem((MODES, 2, SIDE, SIDE), f32),
             vmem((MODES, 2, SIDE, SIDE), f32),
             vmem((SIDE, SIDE), f32),
-            vmem((64, 32, SIDE), f32),
+            vmem((32 * CHUNKS, UNIT, SIDE), f32),
             vmem((SLOTS, PEERS, 32, SIDE), f32),
             vmem((SLOTS, PEERS, 32, SIDE), f32),
             vmem((32, 1024), f32),
             vmem((32, 1024), f32),
-            vmem((2, 16, 32, SIDE), f32),
-            vmem((2, 16, 32, SIDE), f32),
-            vmem((2, 16, 32, SIDE), f32),
-            vmem((2, 8, 32, SIDE), f32),
+            vmem((CHUNKS, 16, UNIT, SIDE), f32),
+            vmem((CHUNKS, 16, UNIT, SIDE), f32),
+            vmem((CHUNKS, 16, UNIT, SIDE), f32),
+            vmem((CHUNKS, 8, UNIT, SIDE), f32),
             dma((4,)), dma((PEERS,)), dma((PEERS,)), dma((2,)), dma((2,)),
             dma((SLOTS, PEERS)), dma((SLOTS, PEERS)), dma((SLOTS, PEERS)), dma((SLOTS, PEERS)),
-            dma((4,)), dma((4,)), dma((4, PEERS)), dma((4, PEERS)), dma((2, 8)), dma((2, 8)),
+            dma((2 * CHUNKS,)), dma((2 * CHUNKS,)), dma((2 * CHUNKS, PEERS)), dma((2 * CHUNKS, PEERS)),
+            dma((CHUNKS, 8)), dma((CHUNKS, 8)),
         ],
         compiler_params=pltpu.CompilerParams(
             collective_id=0, has_side_effects=True, vmem_limit_bytes=53 << 20

time: 90 us -> 81.9 us (0.910)
  Pallas kernels: 83.1 us -> 75 us
    pallas_call x1, Pallas kernels: 83.1 us -> 75 us  [fused(): pl.pallas_call(fused_kernel, out_shape=[jax.ShapeDtypeStruct((32, 1024),...]
where the time goes in v4:
time: 81.9 us; the launch traced here: 81.7 us
  Pallas kernels  75 us (92%)
  local copies, waits for them, and re-layouts  5.41 us (7%)
  between operations  1.3 us (2%)
    pallas_call x1, Pallas kernels, fused(): pl.pallas_call(fused_kernel, out_shape=[jax.ShapeDtypeStruct((32, 1024),...  75 us
    unnamed x8, local copies, waits for them, and re-layouts  5.41 us

profile of v4, /device:TPU:1, one launch (start us, length us, event | category | flops | bytes accessed | tf_op | source)
XLA Modules:
  0.0 81.7 jit_solution(9798393429525049046)
XLA Ops:
  1.3 0.0 copy-start.2
  1.3 0.7 copy-done.2
  2.0 0.0 copy-start
  2.0 0.9 %copy-done = f32[1,1,4,128,128]{4,3,2,1,0:T(8,128)S(1)} copy-done((f32[1,1,4,128,128]{4,3,2,1,0:T(8,128)S(1)}, f32[1,1,4,128,128]{4,3,2,1,0:T(8,128)}, u32[]{:S(2)}) %copy-start) | copy-done | bytes 262168
  2.9 0.0 copy-start.1
  2.9 0.8 %copy-done.1 = bf16[1,2,2,8,1024]{4,3,2,1,0:T(8,128)(2,1)S(1)} copy-done((bf16[1,2,2,8,1024]{4,3,2,1,0:T(8,128)(2,1)S(1)}, bf16[1,2,2,8,1024]{4,3,2,1,0:T(8,128)(2,1)}, u32[]{:S(2)}) %copy-start.1) | copy-done | bytes 65560
  3.7 75.0 %ptychography.1 = (f32[32,1024]{1,0:T(8,128)S(1)}, f32[64,32,128]{2,1,0:T(8,128)}) custom-call(s32[2,4]{1,0:T(2,128)S(1)} %bitcast.10, s32[1,1]{1,0:T(1,128)S(6)} %copy.10.cnt, bf16[32,1024]{1,0:T(8,128)(2,1)S(1)} %bitcast.9, f32[8,2,128,128]{3,2,1,0:T(8,128)} %probe_hbm.1, f32[4,128,128]{2,1,0:T(8,128)S(1)} %bitcast.7, ...), custom_call_target="tpu_custom_call" | custom-call | tf_op jit(solution)/shard_map/ptychography/pallas_call | solution.py:370
  78.8 0.7 copy.11
  79.4 2.3 %copy.12 = f32[8,2,128,128]{3,2,1,0:T(8,128)} copy(f32[8,2,128,128]{3,2,1,0:T(8,128)} %bitcast.11) | data formatting | bytes 2097152
Async XLA Ops:
  1.3 0.7 copy-start.2
  2.0 0.9 %copy-start = (f32[1,1,4,128,128]{4,3,2,1,0:T(8,128)S(1)}, f32[1,1,4,128,128]{4,3,2,1,0:T(8,128)}, u32[]{:S(2)}) copy-start(f32[1,1,4,128,128]{4,3,2,1,0:T(8,128)} %param.10) | copy-start | bytes 786436
  2.9 0.8 %copy-start.1 = (bf16[1,2,2,8,1024]{4,3,2,1,0:T(8,128)(2,1)S(1)}, bf16[1,2,2,8,1024]{4,3,2,1,0:T(8,128)(2,1)}, u32[]{:S(2)}) copy-start(bf16[1,2,2,8,1024]{4,3,2,1,0:T(8,128)(2,1)} %param.6) | copy-start | bytes 196612

commit v5 on v4

--- a/solution.py
+++ b/solution.py
@@ -18,6 +18,7 @@
 SLOTS = 4
 TILES = 16
 MODES = 8
+HALF = 64
 CHUNKS = 2
 UNIT = 64 // CHUNKS
 PARTS = SIDE // UNIT
@@ -47,52 +48,85 @@
     return a, block, b - block * SIDE
 
 
+def parts(t):
+    hi = t.astype(np.float32).astype(ml_dtypes.bfloat16)
+    return hi, (t.astype(np.float32) - hi.astype(np.float32)).astype(ml_dtypes.bfloat16)
+
+
+def real_form(m):
+    return np.block([[m.real, -m.imag], [m.imag, m.real]])
+
+
 def tables(n):
-    k=np.arange(n)
-    f=np.exp(-2j*np.pi*(np.outer(k,k)%n)/n)/math.sqrt(n)
-    fr=((k+n//2)%n-n//2)/n
-    ph=np.exp(-1j*np.pi*24.0*fr**2)
-    a=np.conj(f)@(ph[:,None]*f)
-    out=[]
-    for m in (a,f):
-        right=np.block([[m.real,m.imag],[-m.imag,m.real]]).astype(np.float32)
-        left=np.block([[m.real,-m.imag],[m.imag,m.real]]).astype(np.float32)
-        for t in (right,left):
-            hi=t.astype(ml_dtypes.bfloat16)
-            lo=(t-hi.astype(np.float32)).astype(ml_dtypes.bfloat16)
-            out.append(np.stack([hi,lo]))
-    return np.stack(out)
+    h = n // 2
+    k = np.arange(n)
+    f = np.exp(-2j * np.pi * (np.outer(k, k) % n) / n) / math.sqrt(n)
+    fr = ((k + h) % n - h) / n
+    a = np.conj(f) @ (np.exp(-1j * np.pi * 24.0 * fr ** 2)[:, None] * f)
+    right = np.stack([np.stack(parts(real_form(m).T)) for m in (a, f)])
+    pairs = [
+        ((a[:h, :h] + a[:h, h:]) / 2, (a[:h, :h] - a[:h, h:]) / 2),
+        (f[0::2, :h], f[1::2, :h]),
+        (f[:h, 0::2], f[:h, 1::2]),
+    ]
+    left = []
+    for pair in pairs:
+        for m in pair:
+            hi, lo = parts(real_form(m))
+            left.append(np.block([[hi, hi], [lo, lo]]))
+    return np.stack([*right[0], *right[1], *left])
+
 
 def split(x):
-    hi=x.astype(bf16)
-    return hi,(x-hi.astype(f32)).astype(bf16)
-
-def dot(a,b):
-    return jnp.dot(a,b,preferred_element_type=f32)
-
-
-def two_sided(tab, which, xr, xi):
-    right_hi, right_lo = tab[2 * which, 0], tab[2 * which, 1]
-    left_hi, left_lo = tab[2 * which + 1, 0], tab[2 * which + 1, 1]
-    halves = []
+    hi = x.astype(bf16)
+    return hi, (x - hi.astype(f32)).astype(bf16)
+
+
+def dot(a, b):
+    return jnp.dot(a, b, preferred_element_type=f32)
+
+
+def two_sided(tab, which, kind, xr, xi, before, after):
+    right_hi, right_lo = tab[2 * which], tab[2 * which + 1]
+    left_even, left_odd = tab[4 + 2 * kind], tab[5 + 2 * kind]
+    fields = []
     for m in range(0, MODES, 2):
         rows = [jnp.concatenate([xr[i], xi[i]], axis=1) for i in (m, m + 1)]
         hi, lo = split(jnp.concatenate(rows, axis=0))
-        z = dot(hi, right_hi) + dot(lo, right_hi) + dot(hi, right_lo)
-        top = jnp.concatenate([z[:SIDE, :SIDE], z[SIDE:, :SIDE]], axis=1)
-        bottom = jnp.concatenate([z[:SIDE, SIDE:], z[SIDE:, SIDE:]], axis=1)
-        halves.append(jnp.concatenate([top, bottom], axis=0))
+        fields.append(dot(hi, right_hi) + dot(lo, right_hi) + dot(hi, right_lo))
     real, imag = [], []
-    for half in halves:
-        hi, lo = split(half)
-        o = dot(left_hi, hi) + dot(left_hi, lo) + dot(left_lo, hi)
-        real += [o[:SIDE, :SIDE], o[:SIDE, SIDE:]]
-        imag += [o[SIDE:, :SIDE], o[SIDE:, SIDE:]]
+    for field in fields:
+        quarter = [
+            [
+                jnp.concatenate(
+                    [field[r:r + HALF, p:p + SIDE], field[SIDE + r:SIDE + r + HALF, p:p + SIDE]], axis=1
+                )
+                for r in (0, HALF)
+            ]
+            for p in (0, SIDE)
+        ]
+        if before:
+            even = [first + second for first, second in quarter]
+            odd = [first - second for first, second in quarter]
+        else:
+            even = [first for first, second in quarter]
+            odd = [second for first, second in quarter]
+        sums = []
+        for table, value in ((left_even, even), (left_odd, odd)):
+            hi, lo = split(jnp.concatenate(value, axis=0))
+            o = dot(table, jnp.concatenate([hi, lo], axis=0))
+            sums.append(o[:SIDE] + o[SIDE:])
+        u, v = sums
+        if after:
+            u, v = u + v, u - v
+        for m in (0, SIDE):
+            real.append(jnp.concatenate([u[:HALF, m:m + SIDE], v[:HALF, m:m + SIDE]], axis=0))
+            imag.append(jnp.concatenate([u[HALF:, m:m + SIDE], v[HALF:, m:m + SIDE]], axis=0))
     return real, imag
 
 
-def fused_kernel(off_in, cnt, shard, probe_hbm, pat_hbm, tab_hbm, out, gout,
-                 off, probe, pat, tab, nxt, own_f, nxt_f, wstage, pieces, offs_v, offs,
+def fused_kernel(off_in, cnt, shard_hbm, probe_hbm, pat_hbm, tab_hbm, out, gout,
+                 off, shard, probe, pat, tab, nxt, own_f, nxt_f, wstage, pieces, offs_v, offs,
                  dbl, win, phi, psi, inten, gprobe, gp, gin, nacc, nin,
                  cbuf, work, xybuf, zbuf,
                  local_sem, off_send, off_recv, nxt_send, nxt_recv, win_send, win_recv,
@@ -115,6 +149,8 @@
         pz = lax.rem(z + d, 8)
         return at(x * 4 + lax.rem(pz, 4), y * 4 + lax.div(pz, 4) * 2 + c)
 
+    shard_load = pltpu.make_async_copy(shard_hbm, shard, local_sem.at[4])
+    shard_load.start()
     loads = [
         pltpu.make_async_copy(probe_hbm, probe, local_sem.at[0]),
         pltpu.make_async_copy(tab_hbm, tab, local_sem.at[1]),
@@ -135,6 +171,7 @@
     targets += [at(me, below), at(me, above), partner]
     signal_all(pltpu.get_barrier_semaphore(), targets)
 
+    shard_load.wait()
     first_next = remote(shard, nxt, nxt_send.at[0], nxt_recv.at[0], at(me, below))
     first_next.start()
 
@@ -215,7 +252,7 @@
             pr, pi = probe[m, 0], probe[m, 1]
             xr.append(pr * w0r - pi * w0i)
             xi.append(pr * w0i + pi * w0r)
-        zr, zi = two_sided(tab, 0, xr, xi)
+        zr, zi = two_sided(tab, 0, 0, xr, xi, True, True)
         w1r, w1i = win[2], win[3]
         xr, xi = [], []
         for m in range(MODES):
@@ -223,8 +260,9 @@
             phi[m, 1] = zi[m]
             xr.append(zr[m] * w1r - zi[m] * w1i)
             xi.append(zr[m] * w1i + zi[m] * w1r)
-        zr, zi = two_sided(tab, 1, xr, xi)
-        total = -pat[j]
+        zr, zi = two_sided(tab, 1, 1, xr, xi, True, False)
+        measured = [pat[j, pl.ds(first, HALF, stride=2), :] for first in range(2)]
+        total = -jnp.concatenate(measured, axis=0)
         for m in range(MODES):
             psi[m, 0] = zr[m]
             psi[m, 1] = zi[m]
@@ -237,7 +275,7 @@
         for m in range(MODES):
             xr.append(psi[m, 0] * res)
             xi.append(psi[m, 1] * -res)
-        zr, zi = two_sided(tab, 1, xr, xi)
+        zr, zi = two_sided(tab, 1, 2, xr, xi, False, True)
         w1r, w1i = win[2], win[3]
         ar = ai = jnp.zeros((SIDE, SIDE), f32)
         xr, xi = [], []
@@ -250,7 +288,7 @@
         for half in range(2):
             dbl[2, half * SIDE:(half + 1) * SIDE] = ar
             dbl[3, half * SIDE:(half + 1) * SIDE] = ai
-        zr, zi = two_sided(tab, 0, xr, xi)
+        zr, zi = two_sided(tab, 0, 0, xr, xi, True, True)
         w0r, w0i = win[0], win[1]
         ar = ai = jnp.zeros((SIDE, SIDE), f32)
         for m in range(MODES):
@@ -329,6 +367,9 @@
         core_copy(k).wait()
         work[k] = gprobe[pl.ds(32 * k + 16 * c, 16)] + cbuf[k]
         each_peer(lambda d: xy_copy(k, d).start())
+    for j in range(SLOTS - 1):
+        each_peer(lambda d: object_copy(j, d).wait())
+    accumulate(range(SLOTS - 1))
     for k in range(CHUNKS):
         each_peer(lambda d: xy_copy(k, d).wait())
         total = work[k, index]
@@ -337,9 +378,6 @@
         zbuf[k, z] = total
         for d in range(1, 8):
             z_copy(k, d).start()
-    for j in range(SLOTS - 1):
-        each_peer(lambda d: object_copy(j, d).wait())
-    accumulate(range(SLOTS - 1))
     each_peer(lambda d: object_copy(SLOTS - 1, d).wait())
     accumulate(range(SLOTS - 1, SLOTS))
     last_next = remote(nacc, nin, nxt_send.at[1], nxt_recv.at[1], at(me, above))
@@ -373,13 +411,14 @@
             jax.ShapeDtypeStruct((32, 1024), f32),
             jax.ShapeDtypeStruct((32 * CHUNKS, UNIT, SIDE), f32),
         ],
-        in_specs=[sm, sm, vm, hbm, hbm, hbm],
+        in_specs=[sm, sm, hbm, hbm, hbm, hbm],
         out_specs=[vm, vm],
         scratch_shapes=[
             vmem((1, SIDE), jnp.int32),
+            vmem((32, 1024), bf16),
             vmem((MODES, 2, SIDE, SIDE), f32),
             vmem((SLOTS, SIDE, SIDE), f32),
-            vmem((4, 2, 256, 256), bf16),
+            vmem((10, 256, 256), bf16),
             vmem((32, 1024), bf16),
             vmem((9, 32, SIDE), f32),
             vmem((9, 32, SIDE), f32),
@@ -401,16 +440,16 @@
             vmem((CHUNKS, 16, UNIT, SIDE), f32),
             vmem((CHUNKS, 16, UNIT, SIDE), f32),
             vmem((CHUNKS, 8, UNIT, SIDE), f32),
-            dma((4,)), dma((PEERS,)), dma((PEERS,)), dma((2,)), dma((2,)),
+            dma((5,)), dma((PEERS,)), dma((PEERS,)), dma((2,)), dma((2,)),
             dma((SLOTS, PEERS)), dma((SLOTS, PEERS)), dma((SLOTS, PEERS)), dma((SLOTS, PEERS)),
             dma((2 * CHUNKS,)), dma((2 * CHUNKS,)), dma((2 * CHUNKS, PEERS)), dma((2 * CHUNKS, PEERS)),
             dma((CHUNKS, 8)), dma((CHUNKS, 8)),
         ],
         compiler_params=pltpu.CompilerParams(
-            collective_id=0, has_side_effects=True, vmem_limit_bytes=53 << 20
+            collective_id=0, has_side_effects=True, vmem_limit_bytes=40 << 20
         ),
         name="ptychography",
-    )(offsets, cnt, shard, probe, pat, tab)
+    )(offsets, cnt, *[pltpu.with_memory_space_constraint(v, pltpu.HBM) for v in (shard, probe, pat, tab)])
 
 
 def per_device(object_slices, probe_modes, offsets, counts, patterns):

time: 81.9 us -> 77.7 us (0.949)
  local copies, waits for them, and re-layouts: 5.41 us -> 2.3 us
  Pallas kernels: 75 us -> 74 us
    unnamed x8 -> x4, local copies, waits for them, and re-layouts: 5.41 us -> 2.3 us
    pallas_call x1, Pallas kernels: 75 us -> 74 us  [fused(): pl.pallas_call(fused_kernel, out_shape=[jax.ShapeDtypeStruct((32, 1024),...]
where the time goes in v5:
time: 77.7 us; the launch traced here: 77.6 us
  Pallas kernels  74 us (95%)
  local copies, waits for them, and re-layouts  2.3 us (3%)
  between operations  1.29 us (2%)
    pallas_call x1, Pallas kernels, fused(): pl.pallas_call(fused_kernel, out_shape=[jax.ShapeDtypeStruct((32, 1024),...  74 us
    unnamed x4, local copies, waits for them, and re-layouts  2.3 us

profile of v5, /device:TPU:1, one launch (start us, length us, event | category | flops | bytes accessed | tf_op | source)
XLA Modules:
  0.0 77.6 jit_solution(11124172216958006952)
XLA Ops:
  1.3 0.0 copy-start
  1.3 0.7 copy-done
  2.0 74.0 %ptychography.1 = (f32[32,1024]{1,0:T(8,128)S(1)}, f32[64,32,128]{2,1,0:T(8,128)S(1)}) custom-call(s32[2,4]{1,0:T(2,128)S(1)} %bitcast.9, s32[1,1]{1,0:T(1,128)S(6)} %copy.10.cnt, bf16[32,1024]{1,0:T(8,128)(2,1)} %bitcast.11, f32[8,2,128,128]{3,2,1,0:T(8,128)} %probe_hbm.1, f32[4,128,128]{2,1,0:T(8,128)} %bitcast.10, bf16[10,256,256]{2,1,0:T(8,128)(2,1)} %constant.2.clone.tab_hbm), custom_call_target="tpu_custom_call" | custom-call | tf_op jit(solution)/shard_map/ptychography/pallas_call | solution.py:408
  76.0 0.7 copy.11
  76.7 1.0 %copy.12 = f32[8,2,128,128]{3,2,1,0:T(8,128)} copy(f32[8,2,128,128]{3,2,1,0:T(8,128)S(1)} %bitcast.7) | data formatting | bytes 2097152
Async XLA Ops:
  1.3 0.7 copy-start

commit v6 on v5

--- a/solution.py
+++ b/solution.py
@@ -449,7 +449,7 @@
             collective_id=0, has_side_effects=True, vmem_limit_bytes=40 << 20
         ),
         name="ptychography",
-    )(offsets, cnt, *[pltpu.with_memory_space_constraint(v, pltpu.HBM) for v in (shard, probe, pat, tab)])
+    )(pltpu.with_memory_space_constraint(offsets, pltpu.HBM), cnt, *[pltpu.with_memory_space_constraint(v, pltpu.HBM) for v in (shard, probe, pat, tab)])
 
 
 def per_device(object_slices, probe_modes, offsets, counts, patterns):

time: 77.7 us -> 77.4 us (level)
    unnamed x4 -> x2, local copies, waits for them, and re-layouts: 2.3 us -> 1.63 us
where the time goes in v6:
time: 77.4 us; the launch traced here: 77.3 us
  Pallas kernels  74.4 us (96%)
  local copies, waits for them, and re-layouts  1.63 us (2%)
  between operations  1.29 us (2%)
    pallas_call x1, Pallas kernels, fused(): pl.pallas_call(fused_kernel, out_shape=[jax.ShapeDtypeStruct((32, 1024),...  74.4 us
    unnamed x2, local copies, waits for them, and re-layouts  1.63 us

profile of v6, /device:TPU:1, one launch (start us, length us, event | category | flops | bytes accessed | tf_op | source)
XLA Modules:
  0.0 77.3 jit_solution(15250293024764232050)
XLA Ops:
  1.3 74.4 %ptychography.1 = (f32[32,1024]{1,0:T(8,128)S(1)}, f32[64,32,128]{2,1,0:T(8,128)S(1)}) custom-call(s32[2,4]{1,0:T(2,128)} %bitcast.11, s32[1,1]{1,0:T(1,128)S(6)} %copy.10.cnt, bf16[32,1024]{1,0:T(8,128)(2,1)} %bitcast.10, f32[8,2,128,128]{3,2,1,0:T(8,128)} %probe_hbm.1, f32[4,128,128]{2,1,0:T(8,128)} %bitcast.9, bf16[10,256,256]{2,1,0:T(8,128)(2,1)} %constant.2.clone.tab_hbm), custom_call_target="tpu_custom_call" | custom-call | tf_op jit(solution)/shard_map/ptychography/pallas_call | solution.py:408
  75.7 0.7 copy.11
  76.3 1.0 %copy.12 = f32[8,2,128,128]{3,2,1,0:T(8,128)} copy(f32[8,2,128,128]{3,2,1,0:T(8,128)S(1)} %bitcast.7) | data formatting | bytes 2097152
